TPU v7x, 256 devices: a whole 4x4x8 slice. The times are simulated.
256 devices in a mesh: dp: 32 (over z_hi, x, core), tensor: 8 (over z_lo, y).
Axes of the slice: x: 4, y: 4, z: 8 (z_hi: 4, z_lo: 2; z = z_hi * 2 + z_lo), core: 2. Of those that a mesh axis runs over, the one named last changes fastest.
Arguments:
- gate_pre: bfloat16 [16384, 13312], P('dp', 'tensor'), may hold values from -6 to 6
- up_pre: bfloat16 [16384, 13312], P('dp', 'tensor'), may hold values from -6 to 6
- out_grad: bfloat16 [16384, 5120], P('dp', 'tensor'), may hold values from -0.046875 to 0.046875
- master: float32 [5120, 13312], P('dp', 'tensor'), may hold values from -6 to 6
- moment_one: float32 [5120, 13312], P('dp', 'tensor'), may hold values from -3 to 3
- moment_two: float32 [5120, 13312], P('dp', 'tensor'), may hold values from 0.05 to 1
Outputs:
- master_new: float32 [5120, 13312], P('dp', 'tensor')
- moment_one_new: float32 [5120, 13312], P('dp', 'tensor')
- moment_two_new: float32 [5120, 13312], P('dp', 'tensor')
- serving: bfloat16 [5120, 13312], P(('dp', 'tensor'))
All inputs are finite; a program needn't handle non-finite values.
Results may differ from a plain program's by a relative error of at most 0.006.
Values may be sent and summed in bfloat16 or wider, within the bound.
No kernel may reach another device: no remote copies, remote signals or barrier semaphores. Data moves between devices by JAX's collectives and lax.ppermute only.
A program may use at most 128 MiB of HBM per device.

v0:
```python
import jax
import jax.numpy as jnp
import numpy as np
from jax import lax
from jax.experimental import pallas as pl
from jax.experimental.pallas import tpu as pltpu
from jax.sharding import Mesh, PartitionSpec as P

BF = jnp.bfloat16
F32 = jnp.float32
SIZES = {"zh": 4, "x": 4, "c": 2, "zl": 2, "y": 4}
CHUNKS = ((0, 1024), (1024, 640))
VMEM_LIMIT = 58 * 2**20


def shift(value, axis, by):
    n = SIZES[axis]
    return lax.ppermute(value, axis, [(i, (i + by) % n) for i in range(n)])


def matmul_kernel(where_ref, *refs):
    slabs, pieces = refs[0:9], refs[9:14]
    keep_ref, send_ref, a_all, b_all, sems = refs[14:19]
    copies = []
    for u, slab in enumerate(slabs):
        tokens = slice(0, 4) if u < 7 else slice(2 * u - 14, 2 * u - 12)
        row = pl.multiple_of(where_ref[min(u, 7)], 16)
        copies.append((slab, a_all.at[tokens, pl.ds(row, 160), :]))
    at = 0
    for piece in pieces:
        copies.append((piece, b_all.at[pl.ds(at, piece.shape[0]), :]))
        at += piece.shape[0]
    copies = [
        pltpu.make_async_copy(source, target, sems.at[n])
        for n, (source, target) in enumerate(copies)
    ]
    for copy in copies:
        copy.start()
    for copy in copies:
        copy.wait()

    width = keep_ref.shape[1]
    for m, out_ref in ((0, keep_ref), (640, send_ref)):
        for n in range(0, width, 512):
            cols = slice(n, min(n + 512, width))
            total = None
            for i in range(4):
                part = jnp.dot(
                    a_all[i, m : m + 640, :],
                    b_all[i * 512 : i * 512 + 512, cols],
                    preferred_element_type=F32,
                )
                total = part if total is None else total + part
            out_ref[:, cols] = total.astype(BF)


def matmul(where, slabs, pieces):
    width = pieces[0].shape[1]
    return pl.pallas_call(
        matmul_kernel,
        in_specs=[pl.BlockSpec(memory_space=pltpu.SMEM)]
        + [pl.BlockSpec(memory_space=pltpu.HBM)] * 14,
        scratch_shapes=[
            pltpu.VMEM((4, 1280, 512), BF),
            pltpu.VMEM((2048, width), BF),
            pltpu.SemaphoreType.DMA((14,)),
        ],
        out_shape=[jax.ShapeDtypeStruct((640, width), BF)] * 2,
        compiler_params=pltpu.CompilerParams(vmem_limit_bytes=VMEM_LIMIT),
        cost_estimate=pl.CostEstimate(flops=1, bytes_accessed=1, transcendentals=0),
    )(where, *slabs, *pieces)


def gather_rows(quarters):
    x = lax.axis_index("x")
    pick = lambda by: lax.dynamic_index_in_dim(quarters, (x + by) % 4, 0, keepdims=False)
    return jnp.stack(
        [pick(0), shift(pick(1), "x", 1), shift(pick(3), "x", -1), shift(pick(2), "x", 2)]
    )


def slab_rows():
    zh, c, zl, y = (lax.axis_index(name) for name in ("zh", "c", "zl", "y"))
    where = []
    for z in (zl, 1 - zl):
        for by in (0, 3, 1, 2):
            slab = z * 4 + (y + by) % 4
            where.append((slab // 2 - zh + 4) % 4 * 160 + (slab + c) % 2 * 640)
    return jnp.stack(where).astype(jnp.int32)


def to_owner(rows, by):
    pairs = []
    for z in range(4):
        for i in range(4):
            for j in range(2):
                owner = ((z + by) % 4 * 4 + 2 * j + i // 2) * 2 + i % 2
                pairs.append(((z * 4 + i) * 2 + j, owner))
    return lax.ppermute(rows, ("zh", "x", "c"), pairs)


@jax.named_scope("core_sum")
def fold(keep, send):
    return (keep.astype(F32) + shift(send, "c", 1).astype(F32)).astype(BF)


def plus(a, b):
    return (a.astype(F32) + b.astype(F32)).astype(BF)


def tie(*values):
    return lax.optimization_barrier(values)


@jax.named_scope("relay")
def ring_first(mine):
    return shift(mine[320:400], "zh", 1), shift(mine[400:480], "zh", -1)


@jax.named_scope("to_owner")
def ring_second(mine, far_up, far_down):
    up = jnp.concatenate([plus(mine[160:240], far_up), mine[240:320]], axis=0)
    down = jnp.concatenate([mine[480:560], plus(mine[560:640], far_down)], axis=0)
    return to_owner(up, 1), to_owner(down, -1)


@jax.named_scope("own_to_owner")
def ring_here(mine):
    return to_owner(mine, 0)


def on_device(gate_pre, up_pre, out_grad, master, moment_one, moment_two):
    hidden = []
    for start, width in CHUNKS:
        gate = gate_pre[:, start : start + width].astype(F32)
        up = up_pre[:, start : start + width].astype(F32)
        hidden.append((jax.nn.silu(gate) * up).astype(BF))
    own, *hidden = tie(gather_rows(out_grad.T.reshape(4, 160, 512)), *hidden)
    step = lambda v: (shift(v, "x", 1), shift(v, "x", -1))
    last_step = lambda p, n: (shift(p[:256], "x", 1), shift(n[256:], "x", -1))
    prev0, next0 = step(hidden[0])
    before, after, across, prev0, next0 = tie(
        shift(own, "y", 1), shift(own, "y", -1), shift(own, "zl", 1), prev0, next0
    )
    hidden[1], prev0, next0 = tie(hidden[1], prev0, next0)
    far0 = last_step(prev0, next0)
    prev1, next1 = step(hidden[1])
    opposite, across_before, across_after, *far0 = tie(
        shift(after, "y", -1), shift(across, "y", 1), shift(after, "zl", 1), *far0
    )
    tails = [shift(across_after[:2], "y", -1), shift(across_before[2:], "y", 1)]
    slabs = [own, before, after, opposite, across, across_before, across_after, *tails]
    where = slab_rows()
    keep0, send0 = matmul(where, slabs, [hidden[0], prev0, next0, *far0])
    far1 = last_step(prev1, next1)
    keep0, send0, *far1 = tie(keep0, send0, *far1)
    mine0 = fold(keep0, send0)
    relay0 = ring_first(mine0)
    keep1, send1 = matmul(where, slabs, [hidden[1], prev1, next1, *far1])
    keep1, send1, *relay0 = tie(keep1, send1, *relay0)
    rest0 = ring_second(mine0, *relay0)
    here0, relay0 = tie(mine0[:160], relay0[0])
    here0 = ring_here(here0)
    mine1 = fold(keep1, send1)
    relay1 = ring_first(mine1)
    up1, down1, here1, *rest0 = tie(*relay1, mine1[:160], *rest0)
    here1 = ring_here(here1)
    rest1 = ring_second(mine1, up1, down1)

    total = lambda *values: sum(v.astype(F32) for v in values)
    grad = jnp.concatenate([total(here0, *rest0), total(here1, *rest1)], axis=1)
    moment_one_new = 0.9 * moment_one + 0.1 * grad
    moment_two_new = 0.95 * moment_two + 0.05 * grad * grad
    first = moment_one_new / (1.0 - 0.9**20)
    second = moment_two_new / (1.0 - 0.95**20)
    master_new = master - 0.01 * (first / (jnp.sqrt(second) + 1e-08) + 0.1 * master)
    serving = lax.all_to_all(
        master_new.astype(BF), ("zl", "y"), split_axis=0, concat_axis=1, tiled=True
    )
    return (master_new, moment_one_new, moment_two_new, serving)


def solution(mesh):
    fine = Mesh(mesh.devices.reshape(4, 4, 2, 2, 4), ("zh", "x", "c", "zl", "y"))
    placed = P(("zh", "x", "c"), ("zl", "y"))
    return jax.shard_map(
        on_device,
        mesh=fine,
        in_specs=(placed,) * 6,
        out_specs=(placed, placed, placed, P(("zh", "x", "c", "zl", "y"), None)),
        check_vma=False,
    )
```

profile of v0, /device:TPU:4, one launch (start us, length us, event | category | flops | bytes accessed | tf_op | source)
XLA Modules:
  0.0 168.3 jit_solution(13632995396330775948)
XLA Ops:
  0.7 1.5 copy.13
  2.2 1.3 collective-permute-start
  3.5 0.8 collective-permute-start.1
  4.3 3.5 %collective-permute-start.2 = (bf16[160,512]{1,0:T(8,128)(2,1)S(1)}, bf16[160,512]{1,0:T(8,128)(2,1)S(1)}, u32[]{:S(2)}, u32[]{:S(2)}) collective-permute-start(bf16[160,512]{1,0:T(8,128)(2,1)S(1)} %get-tuple-element.89), channel_id=1, source_target_pairs={{0,32},{16,48},{32,0},{48,16},{1,33},{17,49},{33,1},{49,17},{2,34}... | collective-permute-start | bytes 491528 | tf_op jit(solution)/shard_map/ppermute | solution.py:18
  7.8 1.9 %fusion.4.refs_9_ = bf16[512,1024]{1,0:T(8,128)(2,1)S(1)} fusion(bf16[512,1664]{1,0:T(8,128)(2,1)S(1)} %copy-done.11, bf16[512,1664]{1,0:T(8,128)(2,1)} %param.6), kind=kLoop, calls=%fused_computation.7 | loop fusion | flops 4194304 | bytes 3145728 | tf_op jit(solution)/shard_map/convert_element_type | solution.py:137
  9.7 1.9 %fusion.9.refs_9_ = bf16[512,640]{1,0:T(8,128)(2,1)S(1)} fusion(bf16[512,1664]{1,0:T(8,128)(2,1)S(1)} %copy-done.11, bf16[512,1664]{1,0:T(8,128)(2,1)} %param.6), kind=kLoop, calls=%fused_computation.16 | loop fusion | flops 2621440 | bytes 1966080 | tf_op jit(solution)/shard_map/convert_element_type | solution.py:137
  11.6 0.2 collective-permute-done.2
  11.8 0.1 pad_maximum_fusion.1.refs_0_
  11.9 3.3 %collective-permute-start.6 = (bf16[512,1024]{1,0:T(8,128)(2,1)S(1)}, bf16[512,1024]{1,0:T(8,128)(2,1)S(1)}, u32[]{:S(2)}, u32[]{:S(2)}) collective-permute-start(bf16[512,1024]{1,0:T(8,128)(2,1)S(1)} %fusion.4.refs_9_), channel_id=1, source_target_pairs={{0,16},{16,32},{32,48},{48,0},{1,17},{17,33},{33,49},{49,1},{2,18}... | collective-permute-start | bytes 3145736 | tf_op jit(solution)/shard_map/ppermute | solution.py:18
  15.2 1.0 collective-permute-start.3
  16.1 2.3 %collective-permute-start.4 = (bf16[4,160,512]{2,1,0:T(8,128)(2,1)S(1)}, bf16[4,160,512]{2,1,0:T(8,128)(2,1)S(1)}, u32[]{:S(2)}, u32[]{:S(2)}) collective-permute-start(bf16[4,160,512]{2,1,0:T(8,128)(2,1)S(1)} %pad_maximum_fusion.1.refs_0_), channel_id=1, source_target_pairs={{0,3},{1,0},{2,1},{3,2},{4,7},{5,4},{6,5},{7,6},{8,11},{9,8},{10,9... | collective-permute-start | bytes 1966088 | tf_op jit(solution)/shard_map/ppermute | solution.py:18
  18.4 1.3 collective-permute-start.5
  19.7 11.0 %collective-permute-done.3.refs_1_ = bf16[4,160,512]{2,1,0:T(8,128)(2,1)S(1)} collective-permute-done((bf16[4,160,512]{2,1,0:T(8,128)(2,1)S(1)}, bf16[4,160,512]{2,1,0:T(8,128)(2,1)S(1)}, u32[]{:S(2)}, u32[]{:S(2)}) %collective-permute-start.3) | collective-permute-done | bytes 655392 | tf_op jit(solution)/shard_map/ppermute | solution.py:18
  30.7 1.6 collective-permute-done.5.refs_4_
  32.3 3.7 %collective-permute-done.6.refs_10_ = bf16[512,1024]{1,0:T(8,128)(2,1)S(1)} collective-permute-done((bf16[512,1024]{1,0:T(8,128)(2,1)S(1)}, bf16[512,1024]{1,0:T(8,128)(2,1)S(1)}, u32[]{:S(2)}, u32[]{:S(2)}) %collective-permute-start.6) | collective-permute-done | bytes 1048608 | tf_op jit(solution)/shard_map/ppermute | solution.py:18
  36.1 1.4 collective-permute-done.7.refs_11_
  37.5 2.6 %collective-permute-start.11 = (bf16[256,1024]{1,0:T(8,128)(2,1)S(1)}, bf16[256,1024]{1,0:T(8,128)(2,1)}, u32[]{:S(2)}, u32[]{:S(2)}) collective-permute-start(bf16[256,1024]{1,0:T(8,128)(2,1)S(1)} %slice.76), channel_id=1, source_target_pairs={{0,16},{16,32},{32,48},{48,0},{1,17},{17,33},{33,49},{49,1},{2,18}... | collective-permute-start | bytes 1572872 | tf_op jit(solution)/shard_map/ppermute | solution.py:18
  40.1 0.1 collective-permute-start.12
  40.2 2.8 %collective-permute-start.10 = (bf16[4,160,512]{2,1,0:T(8,128)(2,1)S(1)}, bf16[4,160,512]{2,1,0:T(8,128)(2,1)S(1)}, u32[]{:S(2)}, u32[]{:S(2)}) collective-permute-start(bf16[4,160,512]{2,1,0:T(8,128)(2,1)S(1)} %collective-permute-done.4.refs_2_), channel_id=1, source_target_pairs={{0,4},{4,0},{1,5},{5,1},{2,6},{6,2},{3,7},{7,3},{8,12},{12,8},{9,1... | collective-permute-start | bytes 1966088 | tf_op jit(solution)/shard_map/ppermute | solution.py:18
  43.0 3.0 %collective-permute-start.8 = (bf16[4,160,512]{2,1,0:T(8,128)(2,1)S(1)}, bf16[4,160,512]{2,1,0:T(8,128)(2,1)S(1)}, u32[]{:S(2)}, u32[]{:S(2)}) collective-permute-start(bf16[4,160,512]{2,1,0:T(8,128)(2,1)S(1)} %collective-permute-done.4.refs_2_), channel_id=1, source_target_pairs={{0,3},{1,0},{2,1},{3,2},{4,7},{5,4},{6,5},{7,6},{8,11},{9,8},{10,9... | collective-permute-start | bytes 1966088 | tf_op jit(solution)/shard_map/ppermute | solution.py:18
  46.0 3.6 %collective-permute-done.11.refs_12_ = bf16[256,1024]{1,0:T(8,128)(2,1)} collective-permute-done((bf16[256,1024]{1,0:T(8,128)(2,1)S(1)}, bf16[256,1024]{1,0:T(8,128)(2,1)}, u32[]{:S(2)}, u32[]{:S(2)}) %collective-permute-start.11) | collective-permute-done | bytes 524320 | tf_op jit(solution)/shard_map/ppermute | solution.py:18
  49.6 2.6 %collective-permute-start.15 = (bf16[512,640]{1,0:T(8,128)(2,1)S(1)}, bf16[512,640]{1,0:T(8,128)(2,1)S(1)}, u32[]{:S(2)}, u32[]{:S(2)}) collective-permute-start(bf16[512,640]{1,0:T(8,128)(2,1)S(1)} %fusion.9.refs_9_), channel_id=1, source_target_pairs={{0,16},{16,32},{32,48},{48,0},{1,17},{17,33},{33,49},{49,1},{2,18}... | collective-permute-start | bytes 1966088 | tf_op jit(solution)/shard_map/ppermute | solution.py:18
  52.2 0.3 collective-permute-start.17
  52.5 2.9 %collective-permute-done.10.refs_6_ = bf16[4,160,512]{2,1,0:T(8,128)(2,1)S(1)} collective-permute-done((bf16[4,160,512]{2,1,0:T(8,128)(2,1)S(1)}, bf16[4,160,512]{2,1,0:T(8,128)(2,1)S(1)}, u32[]{:S(2)}, u32[]{:S(2)}) %collective-permute-start.10) | collective-permute-done | bytes 655392 | tf_op jit(solution)/shard_map/ppermute | solution.py:18
  55.4 2.0 %collective-permute-done.8.refs_3_ = bf16[4,160,512]{2,1,0:T(8,128)(2,1)S(1)} collective-permute-done((bf16[4,160,512]{2,1,0:T(8,128)(2,1)S(1)}, bf16[4,160,512]{2,1,0:T(8,128)(2,1)S(1)}, u32[]{:S(2)}, u32[]{:S(2)}) %collective-permute-start.8) | collective-permute-done | bytes 655392 | tf_op jit(solution)/shard_map/ppermute | solution.py:18
  57.4 0.8 copy-done.7
  58.2 2.6 %collective-permute-done.9.refs_5_ = bf16[4,160,512]{2,1,0:T(8,128)(2,1)S(1)} collective-permute-done((bf16[4,160,512]{2,1,0:T(8,128)(2,1)S(1)}, bf16[4,160,512]{2,1,0:T(8,128)(2,1)S(1)}, u32[]{:S(2)}, u32[]{:S(2)}) %collective-permute-start.9) | collective-permute-done | bytes 655392 | tf_op jit(solution)/shard_map/ppermute | solution.py:18
  60.8 0.8 slice.78
  61.6 1.2 collective-permute-start.13
  62.8 1.0 collective-permute-start.14
  63.9 2.4 %collective-permute-start.16 = (bf16[256,640]{1,0:T(8,128)(2,1)S(1)}, bf16[256,640]{1,0:T(8,128)(2,1)S(1)}, u32[]{:S(2)}, u32[]{:S(2)}) collective-permute-start(bf16[256,640]{1,0:T(8,128)(2,1)S(1)} %slice.96), channel_id=1, source_target_pairs={{0,16},{16,32},{32,48},{48,0},{1,17},{17,33},{33,49},{49,1},{2,18}... | collective-permute-start | bytes 983048 | tf_op jit(solution)/shard_map/ppermute | solution.py:18
  66.4 0.8 copy-done.13
  67.2 0.7 stack.48.where_ref
  67.8 1.2 collective-permute-done.13.refs_7_
  69.1 2.1 %collective-permute-done.14.refs_8_ = bf16[2,160,512]{2,1,0:T(8,128)(2,1)S(1)} collective-permute-done((bf16[2,160,512]{2,1,0:T(8,128)(2,1)S(1)}, bf16[2,160,512]{2,1,0:T(8,128)(2,1)S(1)}, u32[]{:S(2)}, u32[]{:S(2)}) %collective-permute-start.14) | collective-permute-done | bytes 327712 | tf_op jit(solution)/shard_map/ppermute | solution.py:18
  71.2 0.7 copy-done.14
  71.9 11.1 %shard_map.93 = (bf16[640,1024]{1,0:T(8,128)(2,1)}, bf16[640,1024]{1,0:T(8,128)(2,1)}) custom-call(s32[8]{0:T(128)} %stack.48.where_ref, bf16[4,160,512]{2,1,0:T(8,128)(2,1)} %copy-done, bf16[4,160,512]{2,1,0:T(8,128)(2,1)} %copy-done.4, bf16[4,160,512]{2,1,0:T(8,128)(2,1)} %copy-done.5, bf16[4,160,512]{2,1,0:T(8,128)(2,1)} %copy-done.7, ...), custom_call_target="tpu_custom_call" | custom-call | flops 1 | bytes 1 | tf_op jit(solution)/shard_map/pallas_call | solution.py:59
  83.1 0.1 collective-permute-start.19
  83.2 3.2 %collective-permute-done.19 = bf16[640,1024]{1,0:T(8,128)(2,1)S(1)} collective-permute-done((bf16[640,1024]{1,0:T(8,128)(2,1)}, bf16[640,1024]{1,0:T(8,128)(2,1)S(1)}, u32[]{:S(2)}, u32[]{:S(2)}) %collective-permute-start.19) | collective-permute-done | bytes 1310752 | tf_op jit(solution)/shard_map/core_sum/ppermute | solution.py:18
  86.4 1.9 %add_convert_fusion = bf16[640,1024]{1,0:T(8,128)(2,1)S(1)} fusion(bf16[640,1024]{1,0:T(8,128)(2,1)S(1)} %collective-permute-done.19, bf16[640,1024]{1,0:T(8,128)(2,1)} %get-tuple-element.56), kind=kLoop, calls=%fused_computation.2 | loop fusion | flops 2621440 | bytes 3932160 | tf_op jit(solution)/shard_map/core_sum/convert_element_type | solution.py:104
  88.4 3.3 %collective-permute-start.20 = (bf16[80,1024]{1,0:T(8,128)(2,1)S(1)}, bf16[80,1024]{1,0:T(8,128)(2,1)S(1)}, u32[]{:S(2)}, u32[]{:S(2)}) collective-permute-start(bf16[80,1024]{1,0:T(8,128)(2,1)S(1)} %get-tuple-element.79), channel_id=1, source_target_pairs={{0,64},{64,128},{128,192},{192,0},{1,65},{65,129},{129,193},{193,1... | collective-permute-start | bytes 491528 | tf_op jit(solution)/shard_map/relay/ppermute | solution.py:18
  91.7 2.2 %collective-permute-start.21 = (bf16[80,1024]{1,0:T(8,128)(2,1)S(1)}, bf16[80,1024]{1,0:T(8,128)(2,1)S(1)}, u32[]{:S(2)}, u32[]{:S(2)}) collective-permute-start(bf16[80,1024]{1,0:T(8,128)(2,1)S(1)} %get-tuple-element.78), channel_id=1, source_target_pairs={{0,192},{64,0},{128,64},{192,128},{1,193},{65,1},{129,65},{193,129... | collective-permute-start | bytes 491528 | tf_op jit(solution)/shard_map/relay/ppermute | solution.py:18
  93.9 9.1 %shard_map.94 = (bf16[640,640]{1,0:T(8,128)(2,1)}, bf16[640,640]{1,0:T(8,128)(2,1)}) custom-call(s32[8]{0:T(128)} %stack.48.where_ref, bf16[4,160,512]{2,1,0:T(8,128)(2,1)} %copy-done, bf16[4,160,512]{2,1,0:T(8,128)(2,1)} %copy-done.4, bf16[4,160,512]{2,1,0:T(8,128)(2,1)} %copy-done.5, bf16[4,160,512]{2,1,0:T(8,128)(2,1)} %copy-done.7, ...), custom_call_target="tpu_custom_call" | custom-call | flops 1 | bytes 1 | tf_op jit(solution)/shard_map/pallas_call | solution.py:59
  103.1 0.3 collective-permute-start.23
  103.4 0.1 add_convert_fusion.2
  103.5 2.6 %collective-permute-start.27 = (bf16[160,1024]{1,0:T(8,128)(2,1)S(1)}, bf16[160,1024]{1,0:T(8,128)(2,1)S(1)}, u32[]{:S(2)}, u32[]{:S(2)}) collective-permute-start(bf16[160,1024]{1,0:T(8,128)(2,1)S(1)} %pad_maximum_fusion.3), channel_id=1, source_target_pairs={{0,192},{8,224},{16,200},{24,232},{32,208},{40,240},{48,216},{56,2... | collective-permute-start | bytes 983048 | tf_op jit(solution)/shard_map/to_owner/ppermute | solution.py:99
  106.1 2.8 %collective-permute-start.26 = (bf16[160,1024]{1,0:T(8,128)(2,1)S(1)}, bf16[160,1024]{1,0:T(8,128)(2,1)S(1)}, u32[]{:S(2)}, u32[]{:S(2)}) collective-permute-start(bf16[160,1024]{1,0:T(8,128)(2,1)S(1)} %pad_maximum_fusion.2), channel_id=1, source_target_pairs={{0,64},{8,96},{16,72},{24,104},{32,80},{40,112},{48,88},{56,120},{... | collective-permute-start | bytes 983048 | tf_op jit(solution)/shard_map/to_owner/ppermute | solution.py:99
  109.0 0.2 add_convert_fusion.1
  109.2 4.7 %collective-permute-start.24 = (bf16[80,640]{1,0:T(8,128)(2,1)S(1)}, bf16[80,640]{1,0:T(8,128)(2,1)S(1)}, u32[]{:S(2)}, u32[]{:S(2)}) collective-permute-start(bf16[80,640]{1,0:T(8,128)(2,1)S(1)} %get-tuple-element.87), channel_id=1, source_target_pairs={{0,64},{64,128},{128,192},{192,0},{1,65},{65,129},{129,193},{193,1... | collective-permute-start | bytes 307208 | tf_op jit(solution)/shard_map/relay/ppermute | solution.py:18
  113.9 2.5 %collective-permute-start.22 = (bf16[160,1024]{1,0:T(8,128)(2,1)S(1)}, bf16[160,1024]{1,0:T(8,128)(2,1)S(1)}, u32[]{:S(2)}, u32[]{:S(2)}) collective-permute-start(bf16[160,1024]{1,0:T(8,128)(2,1)S(1)} %slice.98), channel_id=1, source_target_pairs={{0,0},{8,32},{16,8},{24,40},{32,16},{40,48},{48,24},{56,56},{64,64... | collective-permute-start | bytes 983048 | tf_op jit(solution)/shard_map/own_to_owner/ppermute | solution.py:99
  116.5 11.0 %collective-permute-done.27 = bf16[160,1024]{1,0:T(8,128)(2,1)S(1)} collective-permute-done((bf16[160,1024]{1,0:T(8,128)(2,1)S(1)}, bf16[160,1024]{1,0:T(8,128)(2,1)S(1)}, u32[]{:S(2)}, u32[]{:S(2)}) %collective-permute-start.27) | collective-permute-done | bytes 327712 | tf_op jit(solution)/shard_map/to_owner/ppermute | solution.py:99
  127.5 0.4 collective-permute-done.25
  128.0 3.8 %collective-permute-start.29 = (bf16[160,640]{1,0:T(8,128)(2,1)S(1)}, bf16[160,640]{1,0:T(8,128)(2,1)S(1)}, u32[]{:S(2)}, u32[]{:S(2)}) collective-permute-start(bf16[160,640]{1,0:T(8,128)(2,1)S(1)} %pad_maximum_fusion.4), channel_id=1, source_target_pairs={{0,64},{8,96},{16,72},{24,104},{32,80},{40,112},{48,88},{56,120},{... | collective-permute-start | bytes 614408 | tf_op jit(solution)/shard_map/to_owner/ppermute | solution.py:99
  131.9 1.8 %collective-permute-start.30 = (bf16[160,640]{1,0:T(8,128)(2,1)S(1)}, bf16[160,640]{1,0:T(8,128)(2,1)S(1)}, u32[]{:S(2)}, u32[]{:S(2)}) collective-permute-start(bf16[160,640]{1,0:T(8,128)(2,1)S(1)} %pad_maximum_fusion.5), channel_id=1, source_target_pairs={{0,192},{8,224},{16,200},{24,232},{32,208},{40,240},{48,216},{56,2... | collective-permute-start | bytes 614408 | tf_op jit(solution)/shard_map/to_owner/ppermute | solution.py:99
  133.7 3.3 %collective-permute-start.28 = (bf16[160,640]{1,0:T(8,128)(2,1)S(1)}, bf16[160,640]{1,0:T(8,128)(2,1)S(1)}, u32[]{:S(2)}, u32[]{:S(2)}) collective-permute-start(bf16[160,640]{1,0:T(8,128)(2,1)S(1)} %slice.103), channel_id=1, source_target_pairs={{0,0},{8,32},{16,8},{24,40},{32,16},{40,48},{48,24},{56,56},{64,64... | collective-permute-start | bytes 614408 | tf_op jit(solution)/shard_map/own_to_owner/ppermute | solution.py:99
  137.0 0.1 convert_add_fusion
  137.1 2.8 %collective-permute-done.29 = bf16[160,640]{1,0:T(8,128)(2,1)S(1)} collective-permute-done((bf16[160,640]{1,0:T(8,128)(2,1)S(1)}, bf16[160,640]{1,0:T(8,128)(2,1)S(1)}, u32[]{:S(2)}, u32[]{:S(2)}) %collective-permute-start.29) | collective-permute-done | bytes 204832 | tf_op jit(solution)/shard_map/to_owner/ppermute | solution.py:99
  139.9 6.9 %collective-permute-done.30 = bf16[160,640]{1,0:T(8,128)(2,1)S(1)} collective-permute-done((bf16[160,640]{1,0:T(8,128)(2,1)S(1)}, bf16[160,640]{1,0:T(8,128)(2,1)S(1)}, u32[]{:S(2)}, u32[]{:S(2)}) %collective-permute-start.30) | collective-permute-done | bytes 204832 | tf_op jit(solution)/shard_map/to_owner/ppermute | solution.py:99
  146.8 1.9 %collective-permute-done.28 = bf16[160,640]{1,0:T(8,128)(2,1)S(1)} collective-permute-done((bf16[160,640]{1,0:T(8,128)(2,1)S(1)}, bf16[160,640]{1,0:T(8,128)(2,1)S(1)}, u32[]{:S(2)}, u32[]{:S(2)}) %collective-permute-start.28) | collective-permute-done | bytes 204832 | tf_op jit(solution)/shard_map/own_to_owner/ppermute | solution.py:99
  148.7 0.1 convert_add_fusion.1
  148.8 2.2 %fusion.11 = (bf16[160,1664]{1,0:T(8,128)(2,1)S(1)}, f32[160,1664]{1,0:T(8,128)}, f32[160,1664]{1,0:T(8,128)}, f32[160,1664]{1,0:T(8,128)}) fusion(f32[160,1664]{1,0:T(8,128)S(1)} %copy-done.15, f32[160,640]{1,0:T(8,128)S(1)} %convert_add_fusion.1, f32[160,1024]{1,0:T(8,128)S(1)} %convert_add_fusion, f32[160,1664]{1,0:T(8,128)S(1)} %copy-done.16, ...), kind=kLoop, calls=%fused_computation.36 | loop fusion | flops 4526080 | bytes 7987200 | tf_op jit(solution)/shard_map/convert_element_type | solution.py:178
  151.0 0.1 all_to_all.14
  151.1 16.2 %all_to_all.19 = bf16[8,20,1664]{2,1,0:T(8,128)(2,1)S(1)} all-to-all(bf16[8,20,1664]{2,1,0:T(8,128)(2,1)S(1)} %all_to_all.14), channel_id=1, replica_groups=mesh['zh'=4,'x'=4,'c'=2,'zl'=2,'y'=4] {'zl','y'}, dimensions={0} | all-to-all | bytes 1064960 | tf_op jit(solution)/shard_map/all_to_all | solution.py:177
  167.5 0.9 copy.15
  (76 shorter events, 0.7 us)
Async XLA Ops:
  0.7 7.1 %copy-start.11 = (bf16[512,1664]{1,0:T(8,128)(2,1)S(1)}, bf16[512,1664]{1,0:T(8,128)(2,1)}, u32[]{:S(2)}) copy-start(bf16[512,1664]{1,0:T(8,128)(2,1)} %param.7) | copy-start | bytes 5111812
  2.2 9.3 %collective-permute-start = (bf16[160,512]{1,0:T(8,128)(2,1)S(1)}, bf16[160,512]{1,0:T(8,128)(2,1)S(1)}, u32[]{:S(2)}, u32[]{:S(2)}) collective-permute-start(bf16[160,512]{1,0:T(8,128)(2,1)S(1)} %get-tuple-element.91), channel_id=1, source_target_pairs={{0,16},{16,32},{32,48},{48,0},{1,17},{17,33},{33,49},{49,1},{2,18}... | collective-permute-start | bytes 491528 | tf_op jit(solution)/shard_map/ppermute | solution.py:18
  3.5 8.1 %collective-permute-start.1 = (bf16[160,512]{1,0:T(8,128)(2,1)S(1)}, bf16[160,512]{1,0:T(8,128)(2,1)S(1)}, u32[]{:S(2)}, u32[]{:S(2)}) collective-permute-start(bf16[160,512]{1,0:T(8,128)(2,1)S(1)} %get-tuple-element.90), channel_id=1, source_target_pairs={{0,48},{16,0},{32,16},{48,32},{1,49},{17,1},{33,17},{49,33},{2,50}... | collective-permute-start | bytes 491528 | tf_op jit(solution)/shard_map/ppermute | solution.py:18
  4.3 7.4 %collective-permute-start.2 = (bf16[160,512]{1,0:T(8,128)(2,1)S(1)}, bf16[160,512]{1,0:T(8,128)(2,1)S(1)}, u32[]{:S(2)}, u32[]{:S(2)}) collective-permute-start(bf16[160,512]{1,0:T(8,128)(2,1)S(1)} %get-tuple-element.89), channel_id=1, source_target_pairs={{0,32},{16,48},{32,0},{48,16},{1,33},{17,49},{33,1},{49,17},{2,34}... | collective-permute-start | bytes 491528 | tf_op jit(solution)/shard_map/ppermute | solution.py:18
  9.7 5.5 %copy-start.1 = (bf16[512,1024]{1,0:T(8,128)(2,1)}, bf16[512,1024]{1,0:T(8,128)(2,1)S(1)}, u32[]{:S(2)}) copy-start(bf16[512,1024]{1,0:T(8,128)(2,1)S(1)} %fusion.4.refs_9_) | copy-start | bytes 3145732
  11.6 40.6 %copy-start.8 = (bf16[512,640]{1,0:T(8,128)(2,1)}, bf16[512,640]{1,0:T(8,128)(2,1)S(1)}, u32[]{:S(2)}) copy-start(bf16[512,640]{1,0:T(8,128)(2,1)S(1)} %fusion.9.refs_9_) | copy-start | bytes 1966084
  11.9 49.7 %copy-start = (bf16[4,160,512]{2,1,0:T(8,128)(2,1)}, bf16[4,160,512]{2,1,0:T(8,128)(2,1)S(1)}, u32[]{:S(2)}) copy-start(bf16[4,160,512]{2,1,0:T(8,128)(2,1)S(1)} %pad_maximum_fusion.1.refs_0_) | copy-start | bytes 1966084
  11.9 24.2 %collective-permute-start.6 = (bf16[512,1024]{1,0:T(8,128)(2,1)S(1)}, bf16[512,1024]{1,0:T(8,128)(2,1)S(1)}, u32[]{:S(2)}, u32[]{:S(2)}) collective-permute-start(bf16[512,1024]{1,0:T(8,128)(2,1)S(1)} %fusion.4.refs_9_), channel_id=1, source_target_pairs={{0,16},{16,32},{32,48},{48,0},{1,17},{17,33},{33,49},{49,1},{2,18}... | collective-permute-start | bytes 3145736 | tf_op jit(solution)/shard_map/ppermute | solution.py:18
  15.2 22.3 %collective-permute-start.7 = (bf16[512,1024]{1,0:T(8,128)(2,1)S(1)}, bf16[512,1024]{1,0:T(8,128)(2,1)S(1)}, u32[]{:S(2)}, u32[]{:S(2)}) collective-permute-start(bf16[512,1024]{1,0:T(8,128)(2,1)S(1)} %fusion.4.refs_9_), channel_id=1, source_target_pairs={{0,48},{16,0},{32,16},{48,32},{1,49},{17,1},{33,17},{49,33},{2,50}... | collective-permute-start | bytes 3145736 | tf_op jit(solution)/shard_map/ppermute | solution.py:18
  15.2 15.5 %collective-permute-start.3 = (bf16[4,160,512]{2,1,0:T(8,128)(2,1)S(1)}, bf16[4,160,512]{2,1,0:T(8,128)(2,1)S(1)}, u32[]{:S(2)}, u32[]{:S(2)}) collective-permute-start(bf16[4,160,512]{2,1,0:T(8,128)(2,1)S(1)} %pad_maximum_fusion.1.refs_0_), channel_id=1, source_target_pairs={{0,1},{1,2},{2,3},{3,0},{4,5},{5,6},{6,7},{7,4},{8,9},{9,10},{10,1... | collective-permute-start | bytes 1966088 | tf_op jit(solution)/shard_map/ppermute | solution.py:18
  16.1 14.6 %collective-permute-start.4 = (bf16[4,160,512]{2,1,0:T(8,128)(2,1)S(1)}, bf16[4,160,512]{2,1,0:T(8,128)(2,1)S(1)}, u32[]{:S(2)}, u32[]{:S(2)}) collective-permute-start(bf16[4,160,512]{2,1,0:T(8,128)(2,1)S(1)} %pad_maximum_fusion.1.refs_0_), channel_id=1, source_target_pairs={{0,3},{1,0},{2,1},{3,2},{4,7},{5,4},{6,5},{7,6},{8,11},{9,8},{10,9... | collective-permute-start | bytes 1966088 | tf_op jit(solution)/shard_map/ppermute | solution.py:18
  18.4 13.9 %collective-permute-start.5 = (bf16[4,160,512]{2,1,0:T(8,128)(2,1)S(1)}, bf16[4,160,512]{2,1,0:T(8,128)(2,1)S(1)}, u32[]{:S(2)}, u32[]{:S(2)}) collective-permute-start(bf16[4,160,512]{2,1,0:T(8,128)(2,1)S(1)} %pad_maximum_fusion.1.refs_0_), channel_id=1, source_target_pairs={{0,4},{4,0},{1,5},{5,1},{2,6},{6,2},{3,7},{7,3},{8,12},{12,8},{9,1... | collective-permute-start | bytes 1966088 | tf_op jit(solution)/shard_map/ppermute | solution.py:18
  30.7 30.9 %copy-start.4 = (bf16[4,160,512]{2,1,0:T(8,128)(2,1)}, bf16[4,160,512]{2,1,0:T(8,128)(2,1)S(1)}, u32[]{:S(2)}) copy-start(bf16[4,160,512]{2,1,0:T(8,128)(2,1)S(1)} %collective-permute-done.3.refs_1_) | copy-start | bytes 1966084
  30.7 30.9 %copy-start.5 = (bf16[4,160,512]{2,1,0:T(8,128)(2,1)}, bf16[4,160,512]{2,1,0:T(8,128)(2,1)S(1)}, u32[]{:S(2)}) copy-start(bf16[4,160,512]{2,1,0:T(8,128)(2,1)S(1)} %collective-permute-done.4.refs_2_) | copy-start | bytes 1966084
  32.3 29.3 %copy-start.6 = (bf16[4,160,512]{2,1,0:T(8,128)(2,1)}, bf16[4,160,512]{2,1,0:T(8,128)(2,1)S(1)}, u32[]{:S(2)}) copy-start(bf16[4,160,512]{2,1,0:T(8,128)(2,1)S(1)} %collective-permute-done.5.refs_4_) | copy-start | bytes 1966084
  36.1 30.2 %copy-start.9 = (bf16[512,1024]{1,0:T(8,128)(2,1)}, bf16[512,1024]{1,0:T(8,128)(2,1)S(1)}, u32[]{:S(2)}) copy-start(bf16[512,1024]{1,0:T(8,128)(2,1)S(1)} %collective-permute-done.6.refs_10_) | copy-start | bytes 3145732
  37.5 28.8 %copy-start.10 = (bf16[512,1024]{1,0:T(8,128)(2,1)}, bf16[512,1024]{1,0:T(8,128)(2,1)S(1)}, u32[]{:S(2)}) copy-start(bf16[512,1024]{1,0:T(8,128)(2,1)S(1)} %collective-permute-done.7.refs_11_) | copy-start | bytes 3145732
  37.5 12.1 %collective-permute-start.11 = (bf16[256,1024]{1,0:T(8,128)(2,1)S(1)}, bf16[256,1024]{1,0:T(8,128)(2,1)}, u32[]{:S(2)}, u32[]{:S(2)}) collective-permute-start(bf16[256,1024]{1,0:T(8,128)(2,1)S(1)} %slice.76), channel_id=1, source_target_pairs={{0,16},{16,32},{32,48},{48,0},{1,17},{17,33},{33,49},{49,1},{2,18}... | collective-permute-start | bytes 1572872 | tf_op jit(solution)/shard_map/ppermute | solution.py:18
  40.1 12.1 %collective-permute-start.12 = (bf16[256,1024]{1,0:T(8,128)(2,1)S(1)}, bf16[256,1024]{1,0:T(8,128)(2,1)S(1)}, u32[]{:S(2)}, u32[]{:S(2)}) collective-permute-start(bf16[256,1024]{1,0:T(8,128)(2,1)S(1)} %slice.77), channel_id=1, source_target_pairs={{0,48},{16,0},{32,16},{48,32},{1,49},{17,1},{33,17},{49,33},{2,50}... | collective-permute-start | bytes 1572872 | tf_op jit(solution)/shard_map/ppermute | solution.py:18
  40.2 15.2 %collective-permute-start.10 = (bf16[4,160,512]{2,1,0:T(8,128)(2,1)S(1)}, bf16[4,160,512]{2,1,0:T(8,128)(2,1)S(1)}, u32[]{:S(2)}, u32[]{:S(2)}) collective-permute-start(bf16[4,160,512]{2,1,0:T(8,128)(2,1)S(1)} %collective-permute-done.4.refs_2_), channel_id=1, source_target_pairs={{0,4},{4,0},{1,5},{5,1},{2,6},{6,2},{3,7},{7,3},{8,12},{12,8},{9,1... | collective-permute-start | bytes 1966088 | tf_op jit(solution)/shard_map/ppermute | solution.py:18
  43.0 14.4 %collective-permute-start.8 = (bf16[4,160,512]{2,1,0:T(8,128)(2,1)S(1)}, bf16[4,160,512]{2,1,0:T(8,128)(2,1)S(1)}, u32[]{:S(2)}, u32[]{:S(2)}) collective-permute-start(bf16[4,160,512]{2,1,0:T(8,128)(2,1)S(1)} %collective-permute-done.4.refs_2_), channel_id=1, source_target_pairs={{0,3},{1,0},{2,1},{3,2},{4,7},{5,4},{6,5},{7,6},{8,11},{9,8},{10,9... | collective-permute-start | bytes 1966088 | tf_op jit(solution)/shard_map/ppermute | solution.py:18
  46.0 14.8 %collective-permute-start.9 = (bf16[4,160,512]{2,1,0:T(8,128)(2,1)S(1)}, bf16[4,160,512]{2,1,0:T(8,128)(2,1)S(1)}, u32[]{:S(2)}, u32[]{:S(2)}) collective-permute-start(bf16[4,160,512]{2,1,0:T(8,128)(2,1)S(1)} %collective-permute-done.5.refs_4_), channel_id=1, source_target_pairs={{0,1},{1,2},{2,3},{3,0},{4,5},{5,6},{6,7},{7,4},{8,9},{9,10},{10,1... | collective-permute-start | bytes 1966088 | tf_op jit(solution)/shard_map/ppermute | solution.py:18
  49.6 14.2 %collective-permute-start.15 = (bf16[512,640]{1,0:T(8,128)(2,1)S(1)}, bf16[512,640]{1,0:T(8,128)(2,1)S(1)}, u32[]{:S(2)}, u32[]{:S(2)}) collective-permute-start(bf16[512,640]{1,0:T(8,128)(2,1)S(1)} %fusion.9.refs_9_), channel_id=1, source_target_pairs={{0,16},{16,32},{32,48},{48,0},{1,17},{17,33},{33,49},{49,1},{2,18}... | collective-permute-start | bytes 1966088 | tf_op jit(solution)/shard_map/ppermute | solution.py:18
  52.2 5.2 %copy-start.19 = (bf16[256,1024]{1,0:T(8,128)(2,1)}, bf16[256,1024]{1,0:T(8,128)(2,1)S(1)}, u32[]{:S(2)}) copy-start(bf16[256,1024]{1,0:T(8,128)(2,1)S(1)} %collective-permute-done.12.refs_13_) | copy-start | bytes 1572868
  52.2 14.1 %collective-permute-start.17 = (bf16[512,640]{1,0:T(8,128)(2,1)S(1)}, bf16[512,640]{1,0:T(8,128)(2,1)S(1)}, u32[]{:S(2)}, u32[]{:S(2)}) collective-permute-start(bf16[512,640]{1,0:T(8,128)(2,1)S(1)} %fusion.9.refs_9_), channel_id=1, source_target_pairs={{0,48},{16,0},{32,16},{48,32},{1,49},{17,1},{33,17},{49,33},{2,50}... | collective-permute-start | bytes 1966088 | tf_op jit(solution)/shard_map/ppermute | solution.py:18
  55.4 10.9 %copy-start.2 = (bf16[4,160,512]{2,1,0:T(8,128)(2,1)}, bf16[4,160,512]{2,1,0:T(8,128)(2,1)S(1)}, u32[]{:S(2)}) copy-start(bf16[4,160,512]{2,1,0:T(8,128)(2,1)S(1)} %collective-permute-done.10.refs_6_) | copy-start | bytes 1966084
  57.4 0.8 copy-start.7
  60.8 5.5 %copy-start.3 = (bf16[4,160,512]{2,1,0:T(8,128)(2,1)}, bf16[4,160,512]{2,1,0:T(8,128)(2,1)S(1)}, u32[]{:S(2)}) copy-start(bf16[4,160,512]{2,1,0:T(8,128)(2,1)S(1)} %collective-permute-done.9.refs_5_) | copy-start | bytes 1966084
  61.6 7.5 %collective-permute-start.13 = (bf16[2,160,512]{2,1,0:T(8,128)(2,1)}, bf16[2,160,512]{2,1,0:T(8,128)(2,1)}, u32[]{:S(2)}, u32[]{:S(2)}) collective-permute-start(bf16[2,160,512]{2,1,0:T(8,128)(2,1)} %slice.78), channel_id=1, source_target_pairs={{0,3},{1,0},{2,1},{3,2},{4,7},{5,4},{6,5},{7,6},{8,11},{9,8},{10,9... | collective-permute-start | bytes 983048 | tf_op jit(solution)/shard_map/ppermute | solution.py:18
  62.8 8.4 %collective-permute-start.14 = (bf16[2,160,512]{2,1,0:T(8,128)(2,1)S(1)}, bf16[2,160,512]{2,1,0:T(8,128)(2,1)S(1)}, u32[]{:S(2)}, u32[]{:S(2)}) collective-permute-start(bf16[2,160,512]{2,1,0:T(8,128)(2,1)S(1)} %slice.79), channel_id=1, source_target_pairs={{0,1},{1,2},{2,3},{3,0},{4,5},{5,6},{6,7},{7,4},{8,9},{9,10},{10,1... | collective-permute-start | bytes 983048 | tf_op jit(solution)/shard_map/ppermute | solution.py:18
  63.8 2.5 %copy-start.12 = (bf16[512,640]{1,0:T(8,128)(2,1)}, bf16[512,640]{1,0:T(8,128)(2,1)S(1)}, u32[]{:S(2)}) copy-start(bf16[512,640]{1,0:T(8,128)(2,1)S(1)} %collective-permute-done.15.refs_10_) | copy-start | bytes 1966084
  63.9 19.2 %collective-permute-start.16 = (bf16[256,640]{1,0:T(8,128)(2,1)S(1)}, bf16[256,640]{1,0:T(8,128)(2,1)S(1)}, u32[]{:S(2)}, u32[]{:S(2)}) collective-permute-start(bf16[256,640]{1,0:T(8,128)(2,1)S(1)} %slice.96), channel_id=1, source_target_pairs={{0,16},{16,32},{32,48},{48,0},{1,17},{17,33},{33,49},{49,1},{2,18}... | collective-permute-start | bytes 983048 | tf_op jit(solution)/shard_map/ppermute | solution.py:18
  66.3 0.9 copy-start.13
  67.1 15.9 %collective-permute-start.18 = (bf16[256,640]{1,0:T(8,128)(2,1)S(1)}, bf16[256,640]{1,0:T(8,128)(2,1)S(1)}, u32[]{:S(2)}, u32[]{:S(2)}) collective-permute-start(bf16[256,640]{1,0:T(8,128)(2,1)S(1)} %slice.97), channel_id=1, source_target_pairs={{0,48},{16,0},{32,16},{48,32},{1,49},{17,1},{33,17},{49,33},{2,50}... | collective-permute-start | bytes 983048 | tf_op jit(solution)/shard_map/ppermute | solution.py:18
  71.2 0.7 copy-start.14
  83.1 5.2 %copy-start.20 = (bf16[256,640]{1,0:T(8,128)(2,1)}, bf16[256,640]{1,0:T(8,128)(2,1)S(1)}, u32[]{:S(2)}) copy-start(bf16[256,640]{1,0:T(8,128)(2,1)S(1)} %collective-permute-done.16.refs_12_) | copy-start | bytes 983044
  83.1 5.2 %copy-start.21 = (bf16[256,640]{1,0:T(8,128)(2,1)}, bf16[256,640]{1,0:T(8,128)(2,1)S(1)}, u32[]{:S(2)}) copy-start(bf16[256,640]{1,0:T(8,128)(2,1)S(1)} %collective-permute-done.18.refs_13_) | copy-start | bytes 983044
  83.1 3.3 %collective-permute-start.19 = (bf16[640,1024]{1,0:T(8,128)(2,1)}, bf16[640,1024]{1,0:T(8,128)(2,1)S(1)}, u32[]{:S(2)}, u32[]{:S(2)}) collective-permute-start(bf16[640,1024]{1,0:T(8,128)(2,1)} %get-tuple-element.57), channel_id=1, source_target_pairs={{0,8},{8,0},{1,9},{9,1},{2,10},{10,2},{3,11},{11,3},{4,12},{12,4},... | collective-permute-start | bytes 3932168 | tf_op jit(solution)/shard_map/core_sum/ppermute | solution.py:18
  88.4 14.7 %collective-permute-start.20 = (bf16[80,1024]{1,0:T(8,128)(2,1)S(1)}, bf16[80,1024]{1,0:T(8,128)(2,1)S(1)}, u32[]{:S(2)}, u32[]{:S(2)}) collective-permute-start(bf16[80,1024]{1,0:T(8,128)(2,1)S(1)} %get-tuple-element.79), channel_id=1, source_target_pairs={{0,64},{64,128},{128,192},{192,0},{1,65},{65,129},{129,193},{193,1... | collective-permute-start | bytes 491528 | tf_op jit(solution)/shard_map/relay/ppermute | solution.py:18
  91.7 11.4 %collective-permute-start.21 = (bf16[80,1024]{1,0:T(8,128)(2,1)S(1)}, bf16[80,1024]{1,0:T(8,128)(2,1)S(1)}, u32[]{:S(2)}, u32[]{:S(2)}) collective-permute-start(bf16[80,1024]{1,0:T(8,128)(2,1)S(1)} %get-tuple-element.78), channel_id=1, source_target_pairs={{0,192},{64,0},{128,64},{192,128},{1,193},{65,1},{129,65},{193,129... | collective-permute-start | bytes 491528 | tf_op jit(solution)/shard_map/relay/ppermute | solution.py:18
  103.1 5.9 %copy-start.18 = (bf16[640,640]{1,0:T(8,128)(2,1)S(1)}, bf16[640,640]{1,0:T(8,128)(2,1)}, u32[]{:S(2)}) copy-start(bf16[640,640]{1,0:T(8,128)(2,1)} %get-tuple-element.64) | copy-start | bytes 2457604
  103.1 5.9 %collective-permute-start.23 = (bf16[640,640]{1,0:T(8,128)(2,1)}, bf16[640,640]{1,0:T(8,128)(2,1)S(1)}, u32[]{:S(2)}, u32[]{:S(2)}) collective-permute-start(bf16[640,640]{1,0:T(8,128)(2,1)} %get-tuple-element.65), channel_id=1, source_target_pairs={{0,8},{8,0},{1,9},{9,1},{2,10},{10,2},{3,11},{11,3},{4,12},{12,4},... | collective-permute-start | bytes 2457608 | tf_op jit(solution)/shard_map/core_sum/ppermute | solution.py:18
  103.5 24.0 %collective-permute-start.27 = (bf16[160,1024]{1,0:T(8,128)(2,1)S(1)}, bf16[160,1024]{1,0:T(8,128)(2,1)S(1)}, u32[]{:S(2)}, u32[]{:S(2)}) collective-permute-start(bf16[160,1024]{1,0:T(8,128)(2,1)S(1)} %pad_maximum_fusion.3), channel_id=1, source_target_pairs={{0,192},{8,224},{16,200},{24,232},{32,208},{40,240},{48,216},{56,2... | collective-permute-start | bytes 983048 | tf_op jit(solution)/shard_map/to_owner/ppermute | solution.py:99
  106.1 21.4 %collective-permute-start.26 = (bf16[160,1024]{1,0:T(8,128)(2,1)S(1)}, bf16[160,1024]{1,0:T(8,128)(2,1)S(1)}, u32[]{:S(2)}, u32[]{:S(2)}) collective-permute-start(bf16[160,1024]{1,0:T(8,128)(2,1)S(1)} %pad_maximum_fusion.2), channel_id=1, source_target_pairs={{0,64},{8,96},{16,72},{24,104},{32,80},{40,112},{48,88},{56,120},{... | collective-permute-start | bytes 983048 | tf_op jit(solution)/shard_map/to_owner/ppermute | solution.py:99
  109.2 18.3 %collective-permute-start.24 = (bf16[80,640]{1,0:T(8,128)(2,1)S(1)}, bf16[80,640]{1,0:T(8,128)(2,1)S(1)}, u32[]{:S(2)}, u32[]{:S(2)}) collective-permute-start(bf16[80,640]{1,0:T(8,128)(2,1)S(1)} %get-tuple-element.87), channel_id=1, source_target_pairs={{0,64},{64,128},{128,192},{192,0},{1,65},{65,129},{129,193},{193,1... | collective-permute-start | bytes 307208 | tf_op jit(solution)/shard_map/relay/ppermute | solution.py:18
  113.9 14.0 %collective-permute-start.25 = (bf16[80,640]{1,0:T(8,128)(2,1)S(1)}, bf16[80,640]{1,0:T(8,128)(2,1)S(1)}, u32[]{:S(2)}, u32[]{:S(2)}) collective-permute-start(bf16[80,640]{1,0:T(8,128)(2,1)S(1)} %get-tuple-element.86), channel_id=1, source_target_pairs={{0,192},{64,0},{128,64},{192,128},{1,193},{65,1},{129,65},{193,129... | collective-permute-start | bytes 307208 | tf_op jit(solution)/shard_map/relay/ppermute | solution.py:18
  113.9 23.0 %collective-permute-start.22 = (bf16[160,1024]{1,0:T(8,128)(2,1)S(1)}, bf16[160,1024]{1,0:T(8,128)(2,1)S(1)}, u32[]{:S(2)}, u32[]{:S(2)}) collective-permute-start(bf16[160,1024]{1,0:T(8,128)(2,1)S(1)} %slice.98), channel_id=1, source_target_pairs={{0,0},{8,32},{16,8},{24,40},{32,16},{40,48},{48,24},{56,56},{64,64... | collective-permute-start | bytes 983048 | tf_op jit(solution)/shard_map/own_to_owner/ppermute | solution.py:99
  128.0 20.8 %copy-start.17 = (f32[160,1664]{1,0:T(8,128)S(1)}, f32[160,1664]{1,0:T(8,128)}, u32[]{:S(2)}) copy-start(f32[160,1664]{1,0:T(8,128)} %param.11) | copy-start | bytes 3194884
  128.0 11.9 %collective-permute-start.29 = (bf16[160,640]{1,0:T(8,128)(2,1)S(1)}, bf16[160,640]{1,0:T(8,128)(2,1)S(1)}, u32[]{:S(2)}, u32[]{:S(2)}) collective-permute-start(bf16[160,640]{1,0:T(8,128)(2,1)S(1)} %pad_maximum_fusion.4), channel_id=1, source_target_pairs={{0,64},{8,96},{16,72},{24,104},{32,80},{40,112},{48,88},{56,120},{... | collective-permute-start | bytes 614408 | tf_op jit(solution)/shard_map/to_owner/ppermute | solution.py:99
  131.9 17.0 %copy-start.15 = (f32[160,1664]{1,0:T(8,128)S(1)}, f32[160,1664]{1,0:T(8,128)}, u32[]{:S(2)}) copy-start(f32[160,1664]{1,0:T(8,128)} %param.9) | copy-start | bytes 3194884
  131.9 16.9 %copy-start.16 = (f32[160,1664]{1,0:T(8,128)S(1)}, f32[160,1664]{1,0:T(8,128)}, u32[]{:S(2)}) copy-start(f32[160,1664]{1,0:T(8,128)} %param.10) | copy-start | bytes 3194884
  131.9 14.9 %collective-permute-start.30 = (bf16[160,640]{1,0:T(8,128)(2,1)S(1)}, bf16[160,640]{1,0:T(8,128)(2,1)S(1)}, u32[]{:S(2)}, u32[]{:S(2)}) collective-permute-start(bf16[160,640]{1,0:T(8,128)(2,1)S(1)} %pad_maximum_fusion.5), channel_id=1, source_target_pairs={{0,192},{8,224},{16,200},{24,232},{32,208},{40,240},{48,216},{56,2... | collective-permute-start | bytes 614408 | tf_op jit(solution)/shard_map/to_owner/ppermute | solution.py:99
  133.7 15.0 %collective-permute-start.28 = (bf16[160,640]{1,0:T(8,128)(2,1)S(1)}, bf16[160,640]{1,0:T(8,128)(2,1)S(1)}, u32[]{:S(2)}, u32[]{:S(2)}) collective-permute-start(bf16[160,640]{1,0:T(8,128)(2,1)S(1)} %slice.103), channel_id=1, source_target_pairs={{0,0},{8,32},{16,8},{24,40},{32,16},{40,48},{48,24},{56,56},{64,64... | collective-permute-start | bytes 614408 | tf_op jit(solution)/shard_map/own_to_owner/ppermute | solution.py:99
where the time goes:
time: 169 us; the launch traced here: 168 us
  waiting for transfers between devices  58.7 us (35%)
  starting transfers between devices  56.7 us (34%)
  Pallas kernels  20.2 us (12%)
  blocking collectives  16.2 us (10%)
  other arithmetic  8.56 us (5%)
  local copies, waits for them, and re-layouts  6.82 us (4%)
    ppermute x25, starting transfers between devices, shift(): return lax.ppermute(value, axis, [(i, (i + by) % n) for i in range(n)])  40 us
    ppermute x25, waiting for transfers between devices, shift(): return lax.ppermute(value, axis, [(i, (i + by) % n) for i in range(n)])  36.1 us
    ppermute x6, waiting for transfers between devices, to_owner(): return lax.ppermute(rows, ('zh', 'x', 'c'), pairs)  22.6 us
    pallas_call x2, Pallas kernels, matmul(): pl.pallas_call(matmul_kernel, in_specs=[pl.BlockSpec(memory_space=pltpu.S...  20.2 us
    ppermute x6, starting transfers between devices, to_owner(): return lax.ppermute(rows, ('zh', 'x', 'c'), pairs)  16.8 us
    all_to_all x1, blocking collectives, on_device(): lax.all_to_all(master_new.astype(BF), ('zl', 'y'), split_axis=0, concat_a...  16.2 us
    convert_element_type x2, other arithmetic, on_device(): hidden.append((jax.nn.silu(gate) * up).astype(BF))  3.75 us
    unnamed x46, local copies, waits for them, and re-layouts  3.39 us
  transfers between devices with their start and end apart: 31, of which 17 were waited for; matrix products, arithmetic and copies ran while one was open for 4% of the time, Pallas kernels for 12%

commit v1 on v0

--- a/solution.py
+++ b/solution.py
@@ -168,16 +168,20 @@
     rest1 = ring_second(mine1, up1, down1)
 
     total = lambda *values: sum(v.astype(F32) for v in values)
-    grad = jnp.concatenate([total(here0, *rest0), total(here1, *rest1)], axis=1)
-    moment_one_new = 0.9 * moment_one + 0.1 * grad
-    moment_two_new = 0.95 * moment_two + 0.05 * grad * grad
-    first = moment_one_new / (1.0 - 0.9**20)
-    second = moment_two_new / (1.0 - 0.95**20)
-    master_new = master - 0.01 * (first / (jnp.sqrt(second) + 1e-08) + 0.1 * master)
-    serving = lax.all_to_all(
-        master_new.astype(BF), ("zl", "y"), split_axis=0, concat_axis=1, tiled=True
-    )
-    return (master_new, moment_one_new, moment_two_new, serving)
+
+    def adamw(parts):
+        grad = jnp.concatenate([total(*parts[:3]), total(*parts[3:])], axis=1)
+        moment_one_new = 0.9 * moment_one + 0.1 * grad
+        moment_two_new = 0.95 * moment_two + 0.05 * grad * grad
+        first = moment_one_new / (1.0 - 0.9**20)
+        second = moment_two_new / (1.0 - 0.95**20)
+        master_new = master - 0.01 * (first / (jnp.sqrt(second) + 1e-08) + 0.1 * master)
+        return master_new, moment_one_new, moment_two_new
+
+    parts = [here0, *rest0, here1, *rest1]
+    rows, *parts = tie(adamw(parts)[0].astype(BF), *parts)
+    serving = lax.all_to_all(rows, ("zl", "y"), split_axis=0, concat_axis=1, tiled=True)
+    return (*adamw(parts), serving)
 
 
 def solution(mesh):

time: 169 us -> 173 us (1.024)
  blocking collectives: 16.2 us -> 0 us
  waiting for transfers between devices: 58.7 us -> 65.8 us
  local copies, waits for them, and re-layouts: 6.82 us -> 11.2 us
  other arithmetic: 8.56 us -> 12.6 us
  starting transfers between devices: 56.7 us -> 60.5 us
    all_to_all x1 -> x0, blocking collectives: 16.2 us -> none  [on_device(): lax.all_to_all(master_new.astype(BF), ('zl', 'y'), split_axis=0, concat_a...]
    all_to_all x0 -> x1, waiting for transfers between devices: none -> 6.39 us  [on_device(): lax.all_to_all(rows, ('zl', 'y'), split_axis=0, concat_axis=1, tiled=True)]
    all_to_all x0 -> x1, starting transfers between devices: none -> 4.6 us  [on_device(): lax.all_to_all(rows, ('zl', 'y'), split_axis=0, concat_axis=1, tiled=True)]
    all_to_all x2, local copies, waits for them, and re-layouts: 0.16 us -> 3.12 us  [on_device(): lax.all_to_all(rows, ('zl', 'y'), split_axis=0, concat_axis=1, tiled=True)]
    add x2 -> x4, other arithmetic: 0.23 us -> 2.65 us  [on_device(): total = lambda *values: sum((v.astype(F32) for v in values))]
    sub x0 -> x1, other arithmetic: none -> 2.17 us  [adamw(): master - 0.01 * (first / (jnp.sqrt(second) + 1e-08) + 0.1 * master)]
  transfers between devices with their start and end apart: 31 -> 32, of which waited for: 17 -> 18; matrix products, arithmetic and copies ran while one was open for 4% -> 7% of each run, Pallas kernels for 12% -> 12%
where the time goes in v1:
time: 173 us; the launch traced here: 172 us
  waiting for transfers between devices  65.8 us (38%)
  starting transfers between devices  60.5 us (35%)
  Pallas kernels  20.2 us (12%)
  other arithmetic  12.6 us (7%)
  local copies, waits for them, and re-layouts  11.2 us (6%)
    ppermute x25, starting transfers between devices, shift(): return lax.ppermute(value, axis, [(i, (i + by) % n) for i in range(n)])  39.4 us
    ppermute x25, waiting for transfers between devices, shift(): return lax.ppermute(value, axis, [(i, (i + by) % n) for i in range(n)])  35.8 us
    ppermute x6, waiting for transfers between devices, to_owner(): return lax.ppermute(rows, ('zh', 'x', 'c'), pairs)  23.6 us
    pallas_call x2, Pallas kernels, matmul(): pl.pallas_call(matmul_kernel, in_specs=[pl.BlockSpec(memory_space=pltpu.S...  20.2 us
    ppermute x6, starting transfers between devices, to_owner(): return lax.ppermute(rows, ('zh', 'x', 'c'), pairs)  16.6 us
    all_to_all x1, waiting for transfers between devices, on_device(): lax.all_to_all(rows, ('zl', 'y'), split_axis=0, concat_axis=1, tiled=True)  6.39 us
    all_to_all x1, starting transfers between devices, on_device(): lax.all_to_all(rows, ('zl', 'y'), split_axis=0, concat_axis=1, tiled=True)  4.6 us
    convert_element_type x2, other arithmetic, on_device(): hidden.append((jax.nn.silu(gate) * up).astype(BF))  3.75 us
  transfers between devices with their start and end apart: 32, of which 18 were waited for; matrix products, arithmetic and copies ran while one was open for 7% of the time, Pallas kernels for 12%

profile of v1, /device:TPU:4, one launch (start us, length us, event | category | flops | bytes accessed | tf_op | source)
XLA Modules:
  0.0 171.6 jit_solution(10024658342245948688)
XLA Ops:
  0.7 1.5 copy.13
  2.2 1.3 collective-permute-start
  3.5 0.8 collective-permute-start.1
  4.3 3.5 %collective-permute-start.2 = (bf16[160,512]{1,0:T(8,128)(2,1)S(1)}, bf16[160,512]{1,0:T(8,128)(2,1)S(1)}, u32[]{:S(2)}, u32[]{:S(2)}) collective-permute-start(bf16[160,512]{1,0:T(8,128)(2,1)S(1)} %get-tuple-element.102), channel_id=1, source_target_pairs={{0,32},{16,48},{32,0},{48,16},{1,33},{17,49},{33,1},{49,17},{2,34}... | collective-permute-start | bytes 491528 | tf_op jit(solution)/shard_map/ppermute | solution.py:18
  7.8 1.9 %fusion.4.refs_9_ = bf16[512,1024]{1,0:T(8,128)(2,1)S(1)} fusion(bf16[512,1664]{1,0:T(8,128)(2,1)S(1)} %copy-done.14, bf16[512,1664]{1,0:T(8,128)(2,1)} %param.6), kind=kLoop, calls=%fused_computation.7 | loop fusion | flops 4194304 | bytes 3145728 | tf_op jit(solution)/shard_map/convert_element_type | solution.py:137
  9.7 1.9 %fusion.9.refs_9_ = bf16[512,640]{1,0:T(8,128)(2,1)S(1)} fusion(bf16[512,1664]{1,0:T(8,128)(2,1)S(1)} %copy-done.14, bf16[512,1664]{1,0:T(8,128)(2,1)} %param.6), kind=kLoop, calls=%fused_computation.17 | loop fusion | flops 2621440 | bytes 1966080 | tf_op jit(solution)/shard_map/convert_element_type | solution.py:137
  11.9 3.3 %collective-permute-start.6 = (bf16[512,1024]{1,0:T(8,128)(2,1)S(1)}, bf16[512,1024]{1,0:T(8,128)(2,1)S(1)}, u32[]{:S(2)}, u32[]{:S(2)}) collective-permute-start(bf16[512,1024]{1,0:T(8,128)(2,1)S(1)} %fusion.4.refs_9_), channel_id=1, source_target_pairs={{0,16},{16,32},{32,48},{48,0},{1,17},{17,33},{33,49},{49,1},{2,18}... | collective-permute-start | bytes 3145736 | tf_op jit(solution)/shard_map/ppermute | solution.py:18
  15.2 1.0 collective-permute-start.3
  16.1 2.3 %collective-permute-start.4 = (bf16[4,160,512]{2,1,0:T(8,128)(2,1)S(1)}, bf16[4,160,512]{2,1,0:T(8,128)(2,1)S(1)}, u32[]{:S(2)}, u32[]{:S(2)}) collective-permute-start(bf16[4,160,512]{2,1,0:T(8,128)(2,1)S(1)} %pad_maximum_fusion.2.refs_0_), channel_id=1, source_target_pairs={{0,3},{1,0},{2,1},{3,2},{4,7},{5,4},{6,5},{7,6},{8,11},{9,8},{10,9... | collective-permute-start | bytes 1966088 | tf_op jit(solution)/shard_map/ppermute | solution.py:18
  18.4 1.3 collective-permute-start.5
  19.7 11.0 %collective-permute-done.3.refs_1_ = bf16[4,160,512]{2,1,0:T(8,128)(2,1)S(1)} collective-permute-done((bf16[4,160,512]{2,1,0:T(8,128)(2,1)S(1)}, bf16[4,160,512]{2,1,0:T(8,128)(2,1)S(1)}, u32[]{:S(2)}, u32[]{:S(2)}) %collective-permute-start.3) | collective-permute-done | bytes 655392 | tf_op jit(solution)/shard_map/ppermute | solution.py:18
  30.7 1.6 collective-permute-done.5.refs_4_
  32.3 3.7 %collective-permute-done.6.refs_10_ = bf16[512,1024]{1,0:T(8,128)(2,1)S(1)} collective-permute-done((bf16[512,1024]{1,0:T(8,128)(2,1)S(1)}, bf16[512,1024]{1,0:T(8,128)(2,1)S(1)}, u32[]{:S(2)}, u32[]{:S(2)}) %collective-permute-start.6) | collective-permute-done | bytes 1048608 | tf_op jit(solution)/shard_map/ppermute | solution.py:18
  36.1 1.4 collective-permute-done.7.refs_11_
  37.5 2.6 %collective-permute-start.11 = (bf16[256,1024]{1,0:T(8,128)(2,1)S(1)}, bf16[256,1024]{1,0:T(8,128)(2,1)S(1)}, u32[]{:S(2)}, u32[]{:S(2)}) collective-permute-start(bf16[256,1024]{1,0:T(8,128)(2,1)S(1)} %slice.76), channel_id=1, source_target_pairs={{0,16},{16,32},{32,48},{48,0},{1,17},{17,33},{33,49},{49,1},{2,18}... | collective-permute-start | bytes 1572872 | tf_op jit(solution)/shard_map/ppermute | solution.py:18
  40.2 2.8 %collective-permute-start.10 = (bf16[4,160,512]{2,1,0:T(8,128)(2,1)S(1)}, bf16[4,160,512]{2,1,0:T(8,128)(2,1)S(1)}, u32[]{:S(2)}, u32[]{:S(2)}) collective-permute-start(bf16[4,160,512]{2,1,0:T(8,128)(2,1)S(1)} %collective-permute-done.4.refs_2_), channel_id=1, source_target_pairs={{0,4},{4,0},{1,5},{5,1},{2,6},{6,2},{3,7},{7,3},{8,12},{12,8},{9,1... | collective-permute-start | bytes 1966088 | tf_op jit(solution)/shard_map/ppermute | solution.py:18
  43.0 3.0 %collective-permute-start.8 = (bf16[4,160,512]{2,1,0:T(8,128)(2,1)S(1)}, bf16[4,160,512]{2,1,0:T(8,128)(2,1)S(1)}, u32[]{:S(2)}, u32[]{:S(2)}) collective-permute-start(bf16[4,160,512]{2,1,0:T(8,128)(2,1)S(1)} %collective-permute-done.4.refs_2_), channel_id=1, source_target_pairs={{0,3},{1,0},{2,1},{3,2},{4,7},{5,4},{6,5},{7,6},{8,11},{9,8},{10,9... | collective-permute-start | bytes 1966088 | tf_op jit(solution)/shard_map/ppermute | solution.py:18
  46.0 3.7 %collective-permute-done.11.refs_12_ = bf16[256,1024]{1,0:T(8,128)(2,1)S(1)} collective-permute-done((bf16[256,1024]{1,0:T(8,128)(2,1)S(1)}, bf16[256,1024]{1,0:T(8,128)(2,1)S(1)}, u32[]{:S(2)}, u32[]{:S(2)}) %collective-permute-start.11) | collective-permute-done | bytes 524320 | tf_op jit(solution)/shard_map/ppermute | solution.py:18
  49.7 2.5 %collective-permute-start.15 = (bf16[512,640]{1,0:T(8,128)(2,1)S(1)}, bf16[512,640]{1,0:T(8,128)(2,1)S(1)}, u32[]{:S(2)}, u32[]{:S(2)}) collective-permute-start(bf16[512,640]{1,0:T(8,128)(2,1)S(1)} %fusion.9.refs_9_), channel_id=1, source_target_pairs={{0,16},{16,32},{32,48},{48,0},{1,17},{17,33},{33,49},{49,1},{2,18}... | collective-permute-start | bytes 1966088 | tf_op jit(solution)/shard_map/ppermute | solution.py:18
  52.2 0.3 collective-permute-start.17
  52.5 2.9 %collective-permute-done.10.refs_6_ = bf16[4,160,512]{2,1,0:T(8,128)(2,1)S(1)} collective-permute-done((bf16[4,160,512]{2,1,0:T(8,128)(2,1)S(1)}, bf16[4,160,512]{2,1,0:T(8,128)(2,1)S(1)}, u32[]{:S(2)}, u32[]{:S(2)}) %collective-permute-start.10) | collective-permute-done | bytes 655392 | tf_op jit(solution)/shard_map/ppermute | solution.py:18
  55.4 2.0 %collective-permute-done.8.refs_3_ = bf16[4,160,512]{2,1,0:T(8,128)(2,1)S(1)} collective-permute-done((bf16[4,160,512]{2,1,0:T(8,128)(2,1)S(1)}, bf16[4,160,512]{2,1,0:T(8,128)(2,1)S(1)}, u32[]{:S(2)}, u32[]{:S(2)}) %collective-permute-start.8) | collective-permute-done | bytes 655392 | tf_op jit(solution)/shard_map/ppermute | solution.py:18
  57.4 0.8 copy-done.10
  58.2 2.6 %collective-permute-done.9.refs_5_ = bf16[4,160,512]{2,1,0:T(8,128)(2,1)S(1)} collective-permute-done((bf16[4,160,512]{2,1,0:T(8,128)(2,1)S(1)}, bf16[4,160,512]{2,1,0:T(8,128)(2,1)S(1)}, u32[]{:S(2)}, u32[]{:S(2)}) %collective-permute-start.9) | collective-permute-done | bytes 655392 | tf_op jit(solution)/shard_map/ppermute | solution.py:18
  60.8 0.8 slice.78
  61.6 1.2 collective-permute-start.13
  62.8 0.7 slice.79
  63.6 0.9 collective-permute-start.14
  64.5 0.8 slice.96
  65.3 1.6 collective-permute-start.16
  66.9 0.8 slice.97
  67.7 0.4 collective-permute-start.18
  68.3 0.6 stack.48.where_ref
  69.1 3.1 %collective-permute-done.14.refs_8_ = bf16[2,160,512]{2,1,0:T(8,128)(2,1)} collective-permute-done((bf16[2,160,512]{2,1,0:T(8,128)(2,1)}, bf16[2,160,512]{2,1,0:T(8,128)(2,1)}, u32[]{:S(2)}, u32[]{:S(2)}) %collective-permute-start.14) | collective-permute-done | bytes 327712 | tf_op jit(solution)/shard_map/ppermute | solution.py:18
  72.2 11.1 %shard_map.93 = (bf16[640,1024]{1,0:T(8,128)(2,1)}, bf16[640,1024]{1,0:T(8,128)(2,1)}) custom-call(s32[8]{0:T(128)} %stack.48.where_ref, bf16[4,160,512]{2,1,0:T(8,128)(2,1)} %copy-done, bf16[4,160,512]{2,1,0:T(8,128)(2,1)} %copy-done.7, bf16[4,160,512]{2,1,0:T(8,128)(2,1)} %copy-done.8, bf16[4,160,512]{2,1,0:T(8,128)(2,1)} %copy-done.10, ...), custom_call_target="tpu_custom_call" | custom-call | flops 1 | bytes 1 | tf_op jit(solution)/shard_map/pallas_call | solution.py:59
  83.4 3.2 %collective-permute-done.19 = bf16[640,1024]{1,0:T(8,128)(2,1)S(1)} collective-permute-done((bf16[640,1024]{1,0:T(8,128)(2,1)}, bf16[640,1024]{1,0:T(8,128)(2,1)S(1)}, u32[]{:S(2)}, u32[]{:S(2)}) %collective-permute-start.19) | collective-permute-done | bytes 1310752 | tf_op jit(solution)/shard_map/core_sum/ppermute | solution.py:18
  86.6 1.9 %add_convert_fusion = bf16[640,1024]{1,0:T(8,128)(2,1)S(1)} fusion(bf16[640,1024]{1,0:T(8,128)(2,1)S(1)} %collective-permute-done.19, bf16[640,1024]{1,0:T(8,128)(2,1)} %get-tuple-element.63), kind=kLoop, calls=%fused_computation.2 | loop fusion | flops 2621440 | bytes 3932160 | tf_op jit(solution)/shard_map/core_sum/convert_element_type | solution.py:104
  88.5 3.3 %collective-permute-start.20 = (bf16[80,1024]{1,0:T(8,128)(2,1)S(1)}, bf16[80,1024]{1,0:T(8,128)(2,1)S(1)}, u32[]{:S(2)}, u32[]{:S(2)}) collective-permute-start(bf16[80,1024]{1,0:T(8,128)(2,1)S(1)} %get-tuple-element.92), channel_id=1, source_target_pairs={{0,64},{64,128},{128,192},{192,0},{1,65},{65,129},{129,193},{193,1... | collective-permute-start | bytes 491528 | tf_op jit(solution)/shard_map/relay/ppermute | solution.py:18
  91.9 2.2 %collective-permute-start.21 = (bf16[80,1024]{1,0:T(8,128)(2,1)S(1)}, bf16[80,1024]{1,0:T(8,128)(2,1)S(1)}, u32[]{:S(2)}, u32[]{:S(2)}) collective-permute-start(bf16[80,1024]{1,0:T(8,128)(2,1)S(1)} %get-tuple-element.91), channel_id=1, source_target_pairs={{0,192},{64,0},{128,64},{192,128},{1,193},{65,1},{129,65},{193,129... | collective-permute-start | bytes 491528 | tf_op jit(solution)/shard_map/relay/ppermute | solution.py:18
  94.1 9.1 %shard_map.94 = (bf16[640,640]{1,0:T(8,128)(2,1)}, bf16[640,640]{1,0:T(8,128)(2,1)}) custom-call(s32[8]{0:T(128)} %stack.48.where_ref, bf16[4,160,512]{2,1,0:T(8,128)(2,1)} %copy-done, bf16[4,160,512]{2,1,0:T(8,128)(2,1)} %copy-done.7, bf16[4,160,512]{2,1,0:T(8,128)(2,1)} %copy-done.8, bf16[4,160,512]{2,1,0:T(8,128)(2,1)} %copy-done.10, ...), custom_call_target="tpu_custom_call" | custom-call | flops 1 | bytes 1 | tf_op jit(solution)/shard_map/pallas_call | solution.py:59
  103.3 0.3 collective-permute-start.23
  103.7 2.2 %collective-permute-start.27 = (bf16[160,1024]{1,0:T(8,128)(2,1)S(1)}, bf16[160,1024]{1,0:T(8,128)(2,1)S(1)}, u32[]{:S(2)}, u32[]{:S(2)}) collective-permute-start(bf16[160,1024]{1,0:T(8,128)(2,1)S(1)} %pad_maximum_fusion.4), channel_id=1, source_target_pairs={{0,192},{8,224},{16,200},{24,232},{32,208},{40,240},{48,216},{56,2... | collective-permute-start | bytes 983048 | tf_op jit(solution)/shard_map/to_owner/ppermute | solution.py:99
  106.0 2.7 %collective-permute-start.26 = (bf16[160,1024]{1,0:T(8,128)(2,1)S(1)}, bf16[160,1024]{1,0:T(8,128)(2,1)S(1)}, u32[]{:S(2)}, u32[]{:S(2)}) collective-permute-start(bf16[160,1024]{1,0:T(8,128)(2,1)S(1)} %pad_maximum_fusion.3), channel_id=1, source_target_pairs={{0,64},{8,96},{16,72},{24,104},{32,80},{40,112},{48,88},{56,120},{... | collective-permute-start | bytes 983048 | tf_op jit(solution)/shard_map/to_owner/ppermute | solution.py:99
  108.7 0.2 add_convert_fusion.1
  108.9 4.7 %collective-permute-start.24 = (bf16[80,640]{1,0:T(8,128)(2,1)S(1)}, bf16[80,640]{1,0:T(8,128)(2,1)S(1)}, u32[]{:S(2)}, u32[]{:S(2)}) collective-permute-start(bf16[80,640]{1,0:T(8,128)(2,1)S(1)} %get-tuple-element.100), channel_id=1, source_target_pairs={{0,64},{64,128},{128,192},{192,0},{1,65},{65,129},{129,193},{193,1... | collective-permute-start | bytes 307208 | tf_op jit(solution)/shard_map/relay/ppermute | solution.py:18
  113.6 2.7 %collective-permute-start.22 = (bf16[160,1024]{1,0:T(8,128)(2,1)S(1)}, bf16[160,1024]{1,0:T(8,128)(2,1)S(1)}, u32[]{:S(2)}, u32[]{:S(2)}) collective-permute-start(bf16[160,1024]{1,0:T(8,128)(2,1)S(1)} %slice.98), channel_id=1, source_target_pairs={{0,0},{8,32},{16,8},{24,40},{32,16},{40,48},{48,24},{56,56},{64,64... | collective-permute-start | bytes 983048 | tf_op jit(solution)/shard_map/own_to_owner/ppermute | solution.py:99
  116.4 11.2 %collective-permute-done.27 = bf16[160,1024]{1,0:T(8,128)(2,1)S(1)} collective-permute-done((bf16[160,1024]{1,0:T(8,128)(2,1)S(1)}, bf16[160,1024]{1,0:T(8,128)(2,1)S(1)}, u32[]{:S(2)}, u32[]{:S(2)}) %collective-permute-start.27) | collective-permute-done | bytes 327712 | tf_op jit(solution)/shard_map/to_owner/ppermute | solution.py:99
  127.7 0.2 collective-permute-done.25
  128.0 3.9 %collective-permute-start.29 = (bf16[160,640]{1,0:T(8,128)(2,1)S(1)}, bf16[160,640]{1,0:T(8,128)(2,1)}, u32[]{:S(2)}, u32[]{:S(2)}) collective-permute-start(bf16[160,640]{1,0:T(8,128)(2,1)S(1)} %pad_maximum_fusion.5), channel_id=1, source_target_pairs={{0,64},{8,96},{16,72},{24,104},{32,80},{40,112},{48,88},{56,120},{... | collective-permute-start | bytes 614408 | tf_op jit(solution)/shard_map/to_owner/ppermute | solution.py:99
  132.0 1.9 %collective-permute-start.30 = (bf16[160,640]{1,0:T(8,128)(2,1)S(1)}, bf16[160,640]{1,0:T(8,128)(2,1)}, u32[]{:S(2)}, u32[]{:S(2)}) collective-permute-start(bf16[160,640]{1,0:T(8,128)(2,1)S(1)} %pad_maximum_fusion.6), channel_id=1, source_target_pairs={{0,192},{8,224},{16,200},{24,232},{32,208},{40,240},{48,216},{56,2... | collective-permute-start | bytes 614408 | tf_op jit(solution)/shard_map/to_owner/ppermute | solution.py:99
  133.8 3.1 %collective-permute-start.28 = (bf16[160,640]{1,0:T(8,128)(2,1)S(1)}, bf16[160,640]{1,0:T(8,128)(2,1)S(1)}, u32[]{:S(2)}, u32[]{:S(2)}) collective-permute-start(bf16[160,640]{1,0:T(8,128)(2,1)S(1)} %slice.103), channel_id=1, source_target_pairs={{0,0},{8,32},{16,8},{24,40},{32,16},{40,48},{48,24},{56,56},{64,64... | collective-permute-start | bytes 614408 | tf_op jit(solution)/shard_map/own_to_owner/ppermute | solution.py:99
  137.1 4.4 %collective-permute-done.29 = bf16[160,640]{1,0:T(8,128)(2,1)} collective-permute-done((bf16[160,640]{1,0:T(8,128)(2,1)S(1)}, bf16[160,640]{1,0:T(8,128)(2,1)}, u32[]{:S(2)}, u32[]{:S(2)}) %collective-permute-start.29) | collective-permute-done | bytes 204832 | tf_op jit(solution)/shard_map/to_owner/ppermute | solution.py:99
  141.6 5.0 %collective-permute-done.30 = bf16[160,640]{1,0:T(8,128)(2,1)} collective-permute-done((bf16[160,640]{1,0:T(8,128)(2,1)S(1)}, bf16[160,640]{1,0:T(8,128)(2,1)}, u32[]{:S(2)}, u32[]{:S(2)}) %collective-permute-start.30) | collective-permute-done | bytes 204832 | tf_op jit(solution)/shard_map/to_owner/ppermute | solution.py:99
  146.6 2.8 %collective-permute-done.28 = bf16[160,640]{1,0:T(8,128)(2,1)S(1)} collective-permute-done((bf16[160,640]{1,0:T(8,128)(2,1)S(1)}, bf16[160,640]{1,0:T(8,128)(2,1)S(1)}, u32[]{:S(2)}, u32[]{:S(2)}) %collective-permute-start.28) | collective-permute-done | bytes 204832 | tf_op jit(solution)/shard_map/own_to_owner/ppermute | solution.py:99
  149.4 0.7 copy-done.22
  150.1 1.1 convert_add_fusion.3
  151.2 1.6 subtract_convert_fusion
  152.9 2.0 %all_to_all.14 = bf16[8,20,1664]{2,1,0:T(8,128)(2,1)} reshape(bf16[160,1664]{1,0:T(8,128)(2,1)} %subtract_convert_fusion) | data formatting | bytes 1064960 | tf_op jit(solution)/shard_map/all_to_all | solution.py:183
  154.9 4.6 %all-to-all-start = ((bf16[8,20,1664]{2,1,0:T(8,128)(2,1)}), bf16[8,20,1664]{2,1,0:T(8,128)(2,1)}, u32[]{:S(2)}, u32[]{:S(2)}) async-start(bf16[8,20,1664]{2,1,0:T(8,128)(2,1)} %all_to_all.14), calls=%async_computation | async-start | bytes 1277952 | tf_op jit(solution)/shard_map/all_to_all | solution.py:183
  159.5 1.3 convert_add_fusion.2
  161.0 2.2 %multiply_subtract_fusion = (f32[160,1664]{1,0:T(8,128)}, f32[160,1664]{1,0:T(8,128)}, f32[160,1664]{1,0:T(8,128)}) fusion(f32[160,1664]{1,0:T(8,128)S(1)} %copy-done.1, f32[160,640]{1,0:T(8,128)S(1)} %convert_add_fusion.2, f32[160,1024]{1,0:T(8,128)S(1)} %convert_add_fusion, f32[160,1664]{1,0:T(8,128)S(1)} %copy-done.2, f32[160,1664]{1,0:T(8,128)S(1)} %copy-done.3), kind=kLoop, calls=%fused_computation.27 | loop fusion | flops 4259840 | bytes 7454720 | tf_op jit(solution)/shard_map/sub | solution.py:178
  163.2 6.4 %all-to-all-done = bf16[8,20,1664]{2,1,0:T(8,128)(2,1)} async-done(((bf16[8,20,1664]{2,1,0:T(8,128)(2,1)}), bf16[8,20,1664]{2,1,0:T(8,128)(2,1)}, u32[]{:S(2)}, u32[]{:S(2)}) %all-to-all-start) | async-done | bytes 532512 | tf_op jit(solution)/shard_map/all_to_all | solution.py:183
  169.6 1.1 copy.14
  170.7 0.9 copy.15
  (86 shorter events, 1.7 us)
Async XLA Ops:
  0.7 7.1 %copy-start.14 = (bf16[512,1664]{1,0:T(8,128)(2,1)S(1)}, bf16[512,1664]{1,0:T(8,128)(2,1)}, u32[]{:S(2)}) copy-start(bf16[512,1664]{1,0:T(8,128)(2,1)} %param.7) | copy-start | bytes 5111812
  2.2 9.3 %collective-permute-start = (bf16[160,512]{1,0:T(8,128)(2,1)S(1)}, bf16[160,512]{1,0:T(8,128)(2,1)S(1)}, u32[]{:S(2)}, u32[]{:S(2)}) collective-permute-start(bf16[160,512]{1,0:T(8,128)(2,1)S(1)} %get-tuple-element.104), channel_id=1, source_target_pairs={{0,16},{16,32},{32,48},{48,0},{1,17},{17,33},{33,49},{49,1},{2,18}... | collective-permute-start | bytes 491528 | tf_op jit(solution)/shard_map/ppermute | solution.py:18
  3.5 8.1 %collective-permute-start.1 = (bf16[160,512]{1,0:T(8,128)(2,1)S(1)}, bf16[160,512]{1,0:T(8,128)(2,1)S(1)}, u32[]{:S(2)}, u32[]{:S(2)}) collective-permute-start(bf16[160,512]{1,0:T(8,128)(2,1)S(1)} %get-tuple-element.103), channel_id=1, source_target_pairs={{0,48},{16,0},{32,16},{48,32},{1,49},{17,1},{33,17},{49,33},{2,50}... | collective-permute-start | bytes 491528 | tf_op jit(solution)/shard_map/ppermute | solution.py:18
  4.3 7.4 %collective-permute-start.2 = (bf16[160,512]{1,0:T(8,128)(2,1)S(1)}, bf16[160,512]{1,0:T(8,128)(2,1)S(1)}, u32[]{:S(2)}, u32[]{:S(2)}) collective-permute-start(bf16[160,512]{1,0:T(8,128)(2,1)S(1)} %get-tuple-element.102), channel_id=1, source_target_pairs={{0,32},{16,48},{32,0},{48,16},{1,33},{17,49},{33,1},{49,17},{2,34}... | collective-permute-start | bytes 491528 | tf_op jit(solution)/shard_map/ppermute | solution.py:18
  9.7 5.5 %copy-start.4 = (bf16[512,1024]{1,0:T(8,128)(2,1)}, bf16[512,1024]{1,0:T(8,128)(2,1)S(1)}, u32[]{:S(2)}) copy-start(bf16[512,1024]{1,0:T(8,128)(2,1)S(1)} %fusion.4.refs_9_) | copy-start | bytes 3145732
  11.6 40.6 %copy-start.11 = (bf16[512,640]{1,0:T(8,128)(2,1)}, bf16[512,640]{1,0:T(8,128)(2,1)S(1)}, u32[]{:S(2)}) copy-start(bf16[512,640]{1,0:T(8,128)(2,1)S(1)} %fusion.9.refs_9_) | copy-start | bytes 1966084
  11.9 49.8 %copy-start = (bf16[4,160,512]{2,1,0:T(8,128)(2,1)}, bf16[4,160,512]{2,1,0:T(8,128)(2,1)S(1)}, u32[]{:S(2)}) copy-start(bf16[4,160,512]{2,1,0:T(8,128)(2,1)S(1)} %pad_maximum_fusion.2.refs_0_) | copy-start | bytes 1966084
  11.9 24.2 %collective-permute-start.6 = (bf16[512,1024]{1,0:T(8,128)(2,1)S(1)}, bf16[512,1024]{1,0:T(8,128)(2,1)S(1)}, u32[]{:S(2)}, u32[]{:S(2)}) collective-permute-start(bf16[512,1024]{1,0:T(8,128)(2,1)S(1)} %fusion.4.refs_9_), channel_id=1, source_target_pairs={{0,16},{16,32},{32,48},{48,0},{1,17},{17,33},{33,49},{49,1},{2,18}... | collective-permute-start | bytes 3145736 | tf_op jit(solution)/shard_map/ppermute | solution.py:18
  15.2 22.3 %collective-permute-start.7 = (bf16[512,1024]{1,0:T(8,128)(2,1)S(1)}, bf16[512,1024]{1,0:T(8,128)(2,1)S(1)}, u32[]{:S(2)}, u32[]{:S(2)}) collective-permute-start(bf16[512,1024]{1,0:T(8,128)(2,1)S(1)} %fusion.4.refs_9_), channel_id=1, source_target_pairs={{0,48},{16,0},{32,16},{48,32},{1,49},{17,1},{33,17},{49,33},{2,50}... | collective-permute-start | bytes 3145736 | tf_op jit(solution)/shard_map/ppermute | solution.py:18
  15.2 15.5 %collective-permute-start.3 = (bf16[4,160,512]{2,1,0:T(8,128)(2,1)S(1)}, bf16[4,160,512]{2,1,0:T(8,128)(2,1)S(1)}, u32[]{:S(2)}, u32[]{:S(2)}) collective-permute-start(bf16[4,160,512]{2,1,0:T(8,128)(2,1)S(1)} %pad_maximum_fusion.2.refs_0_), channel_id=1, source_target_pairs={{0,1},{1,2},{2,3},{3,0},{4,5},{5,6},{6,7},{7,4},{8,9},{9,10},{10,1... | collective-permute-start | bytes 1966088 | tf_op jit(solution)/shard_map/ppermute | solution.py:18
  16.1 14.6 %collective-permute-start.4 = (bf16[4,160,512]{2,1,0:T(8,128)(2,1)S(1)}, bf16[4,160,512]{2,1,0:T(8,128)(2,1)S(1)}, u32[]{:S(2)}, u32[]{:S(2)}) collective-permute-start(bf16[4,160,512]{2,1,0:T(8,128)(2,1)S(1)} %pad_maximum_fusion.2.refs_0_), channel_id=1, source_target_pairs={{0,3},{1,0},{2,1},{3,2},{4,7},{5,4},{6,5},{7,6},{8,11},{9,8},{10,9... | collective-permute-start | bytes 1966088 | tf_op jit(solution)/shard_map/ppermute | solution.py:18
  18.4 13.9 %collective-permute-start.5 = (bf16[4,160,512]{2,1,0:T(8,128)(2,1)S(1)}, bf16[4,160,512]{2,1,0:T(8,128)(2,1)S(1)}, u32[]{:S(2)}, u32[]{:S(2)}) collective-permute-start(bf16[4,160,512]{2,1,0:T(8,128)(2,1)S(1)} %pad_maximum_fusion.2.refs_0_), channel_id=1, source_target_pairs={{0,4},{4,0},{1,5},{5,1},{2,6},{6,2},{3,7},{7,3},{8,12},{12,8},{9,1... | collective-permute-start | bytes 1966088 | tf_op jit(solution)/shard_map/ppermute | solution.py:18
  30.7 30.9 %copy-start.7 = (bf16[4,160,512]{2,1,0:T(8,128)(2,1)}, bf16[4,160,512]{2,1,0:T(8,128)(2,1)S(1)}, u32[]{:S(2)}) copy-start(bf16[4,160,512]{2,1,0:T(8,128)(2,1)S(1)} %collective-permute-done.3.refs_1_) | copy-start | bytes 1966084
  30.7 30.9 %copy-start.8 = (bf16[4,160,512]{2,1,0:T(8,128)(2,1)}, bf16[4,160,512]{2,1,0:T(8,128)(2,1)S(1)}, u32[]{:S(2)}) copy-start(bf16[4,160,512]{2,1,0:T(8,128)(2,1)S(1)} %collective-permute-done.4.refs_2_) | copy-start | bytes 1966084
  32.3 29.3 %copy-start.9 = (bf16[4,160,512]{2,1,0:T(8,128)(2,1)}, bf16[4,160,512]{2,1,0:T(8,128)(2,1)S(1)}, u32[]{:S(2)}) copy-start(bf16[4,160,512]{2,1,0:T(8,128)(2,1)S(1)} %collective-permute-done.5.refs_4_) | copy-start | bytes 1966084
  36.1 36.1 %copy-start.12 = (bf16[512,1024]{1,0:T(8,128)(2,1)}, bf16[512,1024]{1,0:T(8,128)(2,1)S(1)}, u32[]{:S(2)}) copy-start(bf16[512,1024]{1,0:T(8,128)(2,1)S(1)} %collective-permute-done.6.refs_10_) | copy-start | bytes 3145732
  37.5 34.7 %copy-start.13 = (bf16[512,1024]{1,0:T(8,128)(2,1)}, bf16[512,1024]{1,0:T(8,128)(2,1)S(1)}, u32[]{:S(2)}) copy-start(bf16[512,1024]{1,0:T(8,128)(2,1)S(1)} %collective-permute-done.7.refs_11_) | copy-start | bytes 3145732
  37.5 12.2 %collective-permute-start.11 = (bf16[256,1024]{1,0:T(8,128)(2,1)S(1)}, bf16[256,1024]{1,0:T(8,128)(2,1)S(1)}, u32[]{:S(2)}, u32[]{:S(2)}) collective-permute-start(bf16[256,1024]{1,0:T(8,128)(2,1)S(1)} %slice.76), channel_id=1, source_target_pairs={{0,16},{16,32},{32,48},{48,0},{1,17},{17,33},{33,49},{49,1},{2,18}... | collective-permute-start | bytes 1572872 | tf_op jit(solution)/shard_map/ppermute | solution.py:18
  40.1 12.1 %collective-permute-start.12 = (bf16[256,1024]{1,0:T(8,128)(2,1)S(1)}, bf16[256,1024]{1,0:T(8,128)(2,1)S(1)}, u32[]{:S(2)}, u32[]{:S(2)}) collective-permute-start(bf16[256,1024]{1,0:T(8,128)(2,1)S(1)} %slice.77), channel_id=1, source_target_pairs={{0,48},{16,0},{32,16},{48,32},{1,49},{17,1},{33,17},{49,33},{2,50}... | collective-permute-start | bytes 1572872 | tf_op jit(solution)/shard_map/ppermute | solution.py:18
  40.2 15.2 %collective-permute-start.10 = (bf16[4,160,512]{2,1,0:T(8,128)(2,1)S(1)}, bf16[4,160,512]{2,1,0:T(8,128)(2,1)S(1)}, u32[]{:S(2)}, u32[]{:S(2)}) collective-permute-start(bf16[4,160,512]{2,1,0:T(8,128)(2,1)S(1)} %collective-permute-done.4.refs_2_), channel_id=1, source_target_pairs={{0,4},{4,0},{1,5},{5,1},{2,6},{6,2},{3,7},{7,3},{8,12},{12,8},{9,1... | collective-permute-start | bytes 1966088 | tf_op jit(solution)/shard_map/ppermute | solution.py:18
  43.0 14.4 %collective-permute-start.8 = (bf16[4,160,512]{2,1,0:T(8,128)(2,1)S(1)}, bf16[4,160,512]{2,1,0:T(8,128)(2,1)S(1)}, u32[]{:S(2)}, u32[]{:S(2)}) collective-permute-start(bf16[4,160,512]{2,1,0:T(8,128)(2,1)S(1)} %collective-permute-done.4.refs_2_), channel_id=1, source_target_pairs={{0,3},{1,0},{2,1},{3,2},{4,7},{5,4},{6,5},{7,6},{8,11},{9,8},{10,9... | collective-permute-start | bytes 1966088 | tf_op jit(solution)/shard_map/ppermute | solution.py:18
  46.0 14.8 %collective-permute-start.9 = (bf16[4,160,512]{2,1,0:T(8,128)(2,1)S(1)}, bf16[4,160,512]{2,1,0:T(8,128)(2,1)S(1)}, u32[]{:S(2)}, u32[]{:S(2)}) collective-permute-start(bf16[4,160,512]{2,1,0:T(8,128)(2,1)S(1)} %collective-permute-done.5.refs_4_), channel_id=1, source_target_pairs={{0,1},{1,2},{2,3},{3,0},{4,5},{5,6},{6,7},{7,4},{8,9},{9,10},{10,1... | collective-permute-start | bytes 1966088 | tf_op jit(solution)/shard_map/ppermute | solution.py:18
  49.7 17.2 %copy-start.23 = (bf16[256,1024]{1,0:T(8,128)(2,1)}, bf16[256,1024]{1,0:T(8,128)(2,1)S(1)}, u32[]{:S(2)}) copy-start(bf16[256,1024]{1,0:T(8,128)(2,1)S(1)} %collective-permute-done.11.refs_12_) | copy-start | bytes 1572868
  49.7 14.8 %collective-permute-start.15 = (bf16[512,640]{1,0:T(8,128)(2,1)S(1)}, bf16[512,640]{1,0:T(8,128)(2,1)S(1)}, u32[]{:S(2)}, u32[]{:S(2)}) collective-permute-start(bf16[512,640]{1,0:T(8,128)(2,1)S(1)} %fusion.9.refs_9_), channel_id=1, source_target_pairs={{0,16},{16,32},{32,48},{48,0},{1,17},{17,33},{33,49},{49,1},{2,18}... | collective-permute-start | bytes 1966088 | tf_op jit(solution)/shard_map/ppermute | solution.py:18
  52.2 5.2 %copy-start.24 = (bf16[256,1024]{1,0:T(8,128)(2,1)}, bf16[256,1024]{1,0:T(8,128)(2,1)S(1)}, u32[]{:S(2)}) copy-start(bf16[256,1024]{1,0:T(8,128)(2,1)S(1)} %collective-permute-done.12.refs_13_) | copy-start | bytes 1572868
  52.2 14.7 %collective-permute-start.17 = (bf16[512,640]{1,0:T(8,128)(2,1)S(1)}, bf16[512,640]{1,0:T(8,128)(2,1)S(1)}, u32[]{:S(2)}, u32[]{:S(2)}) collective-permute-start(bf16[512,640]{1,0:T(8,128)(2,1)S(1)} %fusion.9.refs_9_), channel_id=1, source_target_pairs={{0,48},{16,0},{32,16},{48,32},{1,49},{17,1},{33,17},{49,33},{2,50}... | collective-permute-start | bytes 1966088 | tf_op jit(solution)/shard_map/ppermute | solution.py:18
  55.4 12.3 %copy-start.5 = (bf16[4,160,512]{2,1,0:T(8,128)(2,1)}, bf16[4,160,512]{2,1,0:T(8,128)(2,1)S(1)}, u32[]{:S(2)}) copy-start(bf16[4,160,512]{2,1,0:T(8,128)(2,1)S(1)} %collective-permute-done.10.refs_6_) | copy-start | bytes 1966084
  57.4 0.8 copy-start.10
  60.8 6.9 %copy-start.6 = (bf16[4,160,512]{2,1,0:T(8,128)(2,1)}, bf16[4,160,512]{2,1,0:T(8,128)(2,1)S(1)}, u32[]{:S(2)}) copy-start(bf16[4,160,512]{2,1,0:T(8,128)(2,1)S(1)} %collective-permute-done.9.refs_5_) | copy-start | bytes 1966084
  61.6 7.5 %collective-permute-start.13 = (bf16[2,160,512]{2,1,0:T(8,128)(2,1)}, bf16[2,160,512]{2,1,0:T(8,128)(2,1)}, u32[]{:S(2)}, u32[]{:S(2)}) collective-permute-start(bf16[2,160,512]{2,1,0:T(8,128)(2,1)} %slice.78), channel_id=1, source_target_pairs={{0,3},{1,0},{2,1},{3,2},{4,7},{5,4},{6,5},{7,6},{8,11},{9,8},{10,9... | collective-permute-start | bytes 983048 | tf_op jit(solution)/shard_map/ppermute | solution.py:18
  63.6 8.6 %collective-permute-start.14 = (bf16[2,160,512]{2,1,0:T(8,128)(2,1)}, bf16[2,160,512]{2,1,0:T(8,128)(2,1)}, u32[]{:S(2)}, u32[]{:S(2)}) collective-permute-start(bf16[2,160,512]{2,1,0:T(8,128)(2,1)} %slice.79), channel_id=1, source_target_pairs={{0,1},{1,2},{2,3},{3,0},{4,5},{5,6},{6,7},{7,4},{8,9},{9,10},{10,1... | collective-permute-start | bytes 983048 | tf_op jit(solution)/shard_map/ppermute | solution.py:18
  64.5 3.8 %copy-start.15 = (bf16[512,640]{1,0:T(8,128)(2,1)}, bf16[512,640]{1,0:T(8,128)(2,1)S(1)}, u32[]{:S(2)}) copy-start(bf16[512,640]{1,0:T(8,128)(2,1)S(1)} %collective-permute-done.15.refs_10_) | copy-start | bytes 1966084
  65.3 18.0 %collective-permute-start.16 = (bf16[256,640]{1,0:T(8,128)(2,1)}, bf16[256,640]{1,0:T(8,128)(2,1)}, u32[]{:S(2)}, u32[]{:S(2)}) collective-permute-start(bf16[256,640]{1,0:T(8,128)(2,1)} %slice.96), channel_id=1, source_target_pairs={{0,16},{16,32},{32,48},{48,0},{1,17},{17,33},{33,49},{49,1},{2,18}... | collective-permute-start | bytes 983048 | tf_op jit(solution)/shard_map/ppermute | solution.py:18
  66.9 16.4 %copy-start.16 = (bf16[512,640]{1,0:T(8,128)(2,1)}, bf16[512,640]{1,0:T(8,128)(2,1)S(1)}, u32[]{:S(2)}) copy-start(bf16[512,640]{1,0:T(8,128)(2,1)S(1)} %collective-permute-done.17.refs_11_) | copy-start | bytes 1966084
  67.7 15.6 %collective-permute-start.18 = (bf16[256,640]{1,0:T(8,128)(2,1)}, bf16[256,640]{1,0:T(8,128)(2,1)}, u32[]{:S(2)}, u32[]{:S(2)}) collective-permute-start(bf16[256,640]{1,0:T(8,128)(2,1)} %slice.97), channel_id=1, source_target_pairs={{0,48},{16,0},{32,16},{48,32},{1,49},{17,1},{33,17},{49,33},{2,50}... | collective-permute-start | bytes 983048 | tf_op jit(solution)/shard_map/ppermute | solution.py:18
  83.3 3.3 %collective-permute-start.19 = (bf16[640,1024]{1,0:T(8,128)(2,1)}, bf16[640,1024]{1,0:T(8,128)(2,1)S(1)}, u32[]{:S(2)}, u32[]{:S(2)}) collective-permute-start(bf16[640,1024]{1,0:T(8,128)(2,1)} %get-tuple-element.64), channel_id=1, source_target_pairs={{0,8},{8,0},{1,9},{9,1},{2,10},{10,2},{3,11},{11,3},{4,12},{12,4},... | collective-permute-start | bytes 3932168 | tf_op jit(solution)/shard_map/core_sum/ppermute | solution.py:18
  88.5 14.7 %collective-permute-start.20 = (bf16[80,1024]{1,0:T(8,128)(2,1)S(1)}, bf16[80,1024]{1,0:T(8,128)(2,1)S(1)}, u32[]{:S(2)}, u32[]{:S(2)}) collective-permute-start(bf16[80,1024]{1,0:T(8,128)(2,1)S(1)} %get-tuple-element.92), channel_id=1, source_target_pairs={{0,64},{64,128},{128,192},{192,0},{1,65},{65,129},{129,193},{193,1... | collective-permute-start | bytes 491528 | tf_op jit(solution)/shard_map/relay/ppermute | solution.py:18
  91.9 11.4 %collective-permute-start.21 = (bf16[80,1024]{1,0:T(8,128)(2,1)S(1)}, bf16[80,1024]{1,0:T(8,128)(2,1)S(1)}, u32[]{:S(2)}, u32[]{:S(2)}) collective-permute-start(bf16[80,1024]{1,0:T(8,128)(2,1)S(1)} %get-tuple-element.91), channel_id=1, source_target_pairs={{0,192},{64,0},{128,64},{192,128},{1,193},{65,1},{129,65},{193,129... | collective-permute-start | bytes 491528 | tf_op jit(solution)/shard_map/relay/ppermute | solution.py:18
  103.3 5.4 %copy-start.21 = (bf16[640,640]{1,0:T(8,128)(2,1)S(1)}, bf16[640,640]{1,0:T(8,128)(2,1)}, u32[]{:S(2)}) copy-start(bf16[640,640]{1,0:T(8,128)(2,1)} %get-tuple-element.71) | copy-start | bytes 2457604
  103.3 5.4 %collective-permute-start.23 = (bf16[640,640]{1,0:T(8,128)(2,1)}, bf16[640,640]{1,0:T(8,128)(2,1)S(1)}, u32[]{:S(2)}, u32[]{:S(2)}) collective-permute-start(bf16[640,640]{1,0:T(8,128)(2,1)} %get-tuple-element.72), channel_id=1, source_target_pairs={{0,8},{8,0},{1,9},{9,1},{2,10},{10,2},{3,11},{11,3},{4,12},{12,4},... | collective-permute-start | bytes 2457608 | tf_op jit(solution)/shard_map/core_sum/ppermute | solution.py:18
  103.7 23.9 %collective-permute-start.27 = (bf16[160,1024]{1,0:T(8,128)(2,1)S(1)}, bf16[160,1024]{1,0:T(8,128)(2,1)S(1)}, u32[]{:S(2)}, u32[]{:S(2)}) collective-permute-start(bf16[160,1024]{1,0:T(8,128)(2,1)S(1)} %pad_maximum_fusion.4), channel_id=1, source_target_pairs={{0,192},{8,224},{16,200},{24,232},{32,208},{40,240},{48,216},{56,2... | collective-permute-start | bytes 983048 | tf_op jit(solution)/shard_map/to_owner/ppermute | solution.py:99
  106.0 21.7 %collective-permute-start.26 = (bf16[160,1024]{1,0:T(8,128)(2,1)S(1)}, bf16[160,1024]{1,0:T(8,128)(2,1)S(1)}, u32[]{:S(2)}, u32[]{:S(2)}) collective-permute-start(bf16[160,1024]{1,0:T(8,128)(2,1)S(1)} %pad_maximum_fusion.3), channel_id=1, source_target_pairs={{0,64},{8,96},{16,72},{24,104},{32,80},{40,112},{48,88},{56,120},{... | collective-permute-start | bytes 983048 | tf_op jit(solution)/shard_map/to_owner/ppermute | solution.py:99
  108.9 18.7 %collective-permute-start.24 = (bf16[80,640]{1,0:T(8,128)(2,1)S(1)}, bf16[80,640]{1,0:T(8,128)(2,1)S(1)}, u32[]{:S(2)}, u32[]{:S(2)}) collective-permute-start(bf16[80,640]{1,0:T(8,128)(2,1)S(1)} %get-tuple-element.100), channel_id=1, source_target_pairs={{0,64},{64,128},{128,192},{192,0},{1,65},{65,129},{129,193},{193,1... | collective-permute-start | bytes 307208 | tf_op jit(solution)/shard_map/relay/ppermute | solution.py:18
  113.6 14.3 %collective-permute-start.25 = (bf16[80,640]{1,0:T(8,128)(2,1)S(1)}, bf16[80,640]{1,0:T(8,128)(2,1)S(1)}, u32[]{:S(2)}, u32[]{:S(2)}) collective-permute-start(bf16[80,640]{1,0:T(8,128)(2,1)S(1)} %get-tuple-element.99), channel_id=1, source_target_pairs={{0,192},{64,0},{128,64},{192,128},{1,193},{65,1},{129,65},{193,129... | collective-permute-start | bytes 307208 | tf_op jit(solution)/shard_map/relay/ppermute | solution.py:18
  113.6 23.3 %collective-permute-start.22 = (bf16[160,1024]{1,0:T(8,128)(2,1)S(1)}, bf16[160,1024]{1,0:T(8,128)(2,1)S(1)}, u32[]{:S(2)}, u32[]{:S(2)}) collective-permute-start(bf16[160,1024]{1,0:T(8,128)(2,1)S(1)} %slice.98), channel_id=1, source_target_pairs={{0,0},{8,32},{16,8},{24,40},{32,16},{40,48},{48,24},{56,56},{64,64... | collective-permute-start | bytes 983048 | tf_op jit(solution)/shard_map/own_to_owner/ppermute | solution.py:99
  127.7 9.4 %copy-start.17 = (bf16[160,1024]{1,0:T(8,128)(2,1)}, bf16[160,1024]{1,0:T(8,128)(2,1)S(1)}, u32[]{:S(2)}) copy-start(bf16[160,1024]{1,0:T(8,128)(2,1)S(1)} %collective-permute-done.26) | copy-start | bytes 983044
  127.9 23.3 %copy-start.3 = (f32[160,1664]{1,0:T(8,128)S(1)}, f32[160,1664]{1,0:T(8,128)}, u32[]{:S(2)}) copy-start(f32[160,1664]{1,0:T(8,128)} %param.11) | copy-start | bytes 3194884
  128.0 13.6 %collective-permute-start.29 = (bf16[160,640]{1,0:T(8,128)(2,1)S(1)}, bf16[160,640]{1,0:T(8,128)(2,1)}, u32[]{:S(2)}, u32[]{:S(2)}) collective-permute-start(bf16[160,640]{1,0:T(8,128)(2,1)S(1)} %pad_maximum_fusion.5), channel_id=1, source_target_pairs={{0,64},{8,96},{16,72},{24,104},{32,80},{40,112},{48,88},{56,120},{... | collective-permute-start | bytes 614408 | tf_op jit(solution)/shard_map/to_owner/ppermute | solution.py:99
  131.9 19.3 %copy-start.1 = (f32[160,1664]{1,0:T(8,128)S(1)}, f32[160,1664]{1,0:T(8,128)}, u32[]{:S(2)}) copy-start(f32[160,1664]{1,0:T(8,128)} %param.9) | copy-start | bytes 3194884
  132.0 19.3 %copy-start.2 = (f32[160,1664]{1,0:T(8,128)S(1)}, f32[160,1664]{1,0:T(8,128)}, u32[]{:S(2)}) copy-start(f32[160,1664]{1,0:T(8,128)} %param.10) | copy-start | bytes 3194884
  132.0 14.6 %collective-permute-start.30 = (bf16[160,640]{1,0:T(8,128)(2,1)S(1)}, bf16[160,640]{1,0:T(8,128)(2,1)}, u32[]{:S(2)}, u32[]{:S(2)}) collective-permute-start(bf16[160,640]{1,0:T(8,128)(2,1)S(1)} %pad_maximum_fusion.6), channel_id=1, source_target_pairs={{0,192},{8,224},{16,200},{24,232},{32,208},{40,240},{48,216},{56,2... | collective-permute-start | bytes 614408 | tf_op jit(solution)/shard_map/to_owner/ppermute | solution.py:99
  133.8 15.6 %collective-permute-start.28 = (bf16[160,640]{1,0:T(8,128)(2,1)S(1)}, bf16[160,640]{1,0:T(8,128)(2,1)S(1)}, u32[]{:S(2)}, u32[]{:S(2)}) collective-permute-start(bf16[160,640]{1,0:T(8,128)(2,1)S(1)} %slice.103), channel_id=1, source_target_pairs={{0,0},{8,32},{16,8},{24,40},{32,16},{40,48},{48,24},{56,56},{64,64... | collective-permute-start | bytes 614408 | tf_op jit(solution)/shard_map/own_to_owner/ppermute | solution.py:99
  136.9 14.3 %copy-start.19 = (bf16[160,1024]{1,0:T(8,128)(2,1)}, bf16[160,1024]{1,0:T(8,128)(2,1)S(1)}, u32[]{:S(2)}) copy-start(bf16[160,1024]{1,0:T(8,128)(2,1)S(1)} %collective-permute-done.22) | copy-start | bytes 983044
  149.4 0.7 copy-start.22
  154.9 14.7 %all-to-all-start = ((bf16[8,20,1664]{2,1,0:T(8,128)(2,1)}), bf16[8,20,1664]{2,1,0:T(8,128)(2,1)}, u32[]{:S(2)}, u32[]{:S(2)}) async-start(bf16[8,20,1664]{2,1,0:T(8,128)(2,1)} %all_to_all.14), calls=%async_computation | async-start | bytes 1277952 | tf_op jit(solution)/shard_map/all_to_all | solution.py:183
  159.5 1.3 copy-start.18
  159.5 1.4 copy-start.20
